TPU v7x, 32 devices: a whole 2x2x4 slice. The times are simulated.
32 devices in a mesh: blk: 4 (over z), bank: 8 (over y, x, core).
Axes of the slice: x: 2, y: 2, z: 4, core: 2. Of those that a mesh axis runs over, the one named last changes fastest.
Arguments:
- log_density: bfloat16 [128, 32768], P(('blk', 'bank')), may hold values from -8 to 8
- assignment: int32 [128], P(('blk', 'bank')), may hold values from 0 to 7, as said below
Outputs:
- centers: bfloat16 [8, 32768], P(None, 'bank')
- potentials: float32 [128, 32768], P(('blk', 'bank'))
Inputs may be any that keep to these rules, and one draw needn't show every extreme that they name: Every barycenter index is the assignment of at least one member.
All inputs are finite; a program needn't handle non-finite values.
Results may differ from a plain program's by a relative error of at most 0.0051.
Values may be sent and summed in bfloat16 or wider, within the bound.
A program may use at most 64 MiB of HBM per device.

v0:
```python
import jax
import jax.numpy as jnp
from jax import lax
from jax.sharding import PartitionSpec as P

G = 32
BARS = 8
ITERS = 2


def kernel_tables():
    grid_pos = jnp.arange(G, dtype=jnp.float32)
    offset = grid_pos[:, None] - grid_pos[None, :]
    kernel_line = jnp.exp(-0.5 * offset * offset)
    kernel_pair = (
        (kernel_line[:, None, :, None] * kernel_line[None, :, None, :])
        .reshape(G * G, G * G)
        .astype(jnp.bfloat16)
    )
    return (kernel_line, kernel_pair)


def log_convolve(field_log, kernel_line, kernel_pair):
    member_count = field_log.shape[0]
    raised = jnp.exp(field_log).astype(jnp.bfloat16).reshape(member_count * G, G * G)
    inner_sum = jnp.dot(raised, kernel_pair, preferred_element_type=jnp.float32).reshape(
        member_count, G, G * G
    )
    outer_sum = jnp.einsum("ij,mjc->mic", kernel_line, inner_sum, precision=lax.Precision.HIGHEST)
    return jnp.log(outer_sum).reshape(member_count, G * G * G)


def per_device(log_density, assignment):
    kernel_line, kernel_pair = kernel_tables()
    member_count = log_density.shape[0]
    cell_count = log_density.shape[1]
    row_count = cell_count // 128
    labels = jnp.arange(BARS, dtype=jnp.int32)
    onehot = (assignment[:, None] == labels[None, :]).astype(jnp.float32)
    counts = lax.psum(jnp.sum(onehot, axis=0), ("blk", "bank"))
    selector = onehot.astype(jnp.bfloat16)
    member_weights = jnp.transpose(onehot)
    potential = jnp.zeros((member_count, cell_count), jnp.float32)
    center_owned = jnp.zeros((row_count // lax.axis_size("bank"), BARS, 128), jnp.bfloat16)
    for iteration in range(ITERS):
        source = log_density.astype(jnp.float32) - log_convolve(potential, kernel_line, kernel_pair)
        smoothed = log_convolve(source, kernel_line, kernel_pair)
        blocks = smoothed.reshape(member_count, row_count, 128)
        reduced = lax.psum_scatter(
            jnp.einsum("km,mrl->rkl", member_weights, blocks, precision=lax.Precision.HIGHEST),
            "bank",
            scatter_dimension=0,
            tiled=True,
        )
        summed = lax.psum(reduced, "blk")
        center_slice = (summed / counts[None, :, None]).astype(jnp.bfloat16)
        center_all = lax.all_gather(center_slice, "bank", axis=0, tiled=True)
        center_owned = center_slice
        chosen = jnp.einsum("mk,rkl->mrl", selector, center_all, preferred_element_type=jnp.float32)
        potential = chosen.reshape(member_count, cell_count) - smoothed
    centers = jnp.transpose(center_owned, (1, 0, 2)).reshape(BARS, center_owned.shape[0] * 128)
    return (centers, potential)


def solution(mesh):
    placed = (P(("blk", "bank"), None), P(("blk", "bank")))
    return jax.shard_map(
        per_device,
        mesh=mesh,
        in_specs=placed,
        out_specs=(P(None, "bank"), P(("blk", "bank"), None)),
        check_vma=False,
    )
```

profile of v0, /device:TPU:0, one launch (start us, length us, event | category | flops | bytes accessed | tf_op | source)
XLA Modules:
  0.0 217.1 jit_solution(487757982965973390)
XLA Ops:
  7.2 5.3 %multiply_convert_fusion = bf16[32,32,32,32]{3,2,1,0:T(8,128)(2,1)} fusion(f32[32,32]{1,0:T(8,128)S(1)} %fusion.19), kind=kLoop, calls=%fused_computation.2 | loop fusion | flops 2097152 | bytes 2101248 | tf_op jit(solution)/shard_map/convert_element_type | solution.py:18
  12.5 11.3 %reshape.101 = bf16[1024,1024,1]{1,0,2:T(8,128)(2,1)S(1)} reshape(bf16[32,32,32,32]{3,2,1,0:T(8,128)(2,1)} %multiply_convert_fusion) | data formatting | bytes 4194304 | tf_op jit(solution)/shard_map/convert_element_type | solution.py:18
  23.8 0.4 fusion.17
  24.3 0.6 fusion.3
  24.9 0.3 copy.9
  25.2 0.2 fusion.5
  25.5 0.5 fusion.14
  25.9 0.6 fusion.2
  26.5 0.1 reshape_reshape.6
  26.6 2.0 convolution_bitcast_fusion.2
  28.7 38.8 %reduce-scatter.3.cloned.1.call-done = f32[32,8,128]{2,1,0:T(8,128)} async-done(((f32[256,8,128]{2,1,0:T(8,128)}), f32[32,8,128]{2,1,0:T(8,128)}) %reduce-scatter.3.cloned.1.call-update) | async-done | bytes 131088 | tf_op jit(solution)/shard_map/reduce_scatter | solution.py:49
  67.6 0.1 convert_reduce_fusion
  67.6 39.4 %psum.22 = f32[8]{0:T(128)S(1)} all-reduce(f32[8]{0:T(128)S(1)} %convert_reduce_fusion), channel_id=1, replica_groups=mesh['blk'=4,'bank'=8] {'blk','bank'}, use_global_device_ids=true, to_apply=%region_3.0 | all-reduce | flops 8 | bytes 64 | tf_op jit(solution)/shard_map/psum | solution.py:40
  107.0 1.0 divide_convert_fusion.1
  108.0 10.8 %all_gather.6 = bf16[256,8,128]{2,1,0:T(8,128)(2,1)S(1)} all-gather(bf16[32,8,128]{2,1,0:T(8,128)(2,1)S(1)} %divide_convert_fusion.1), channel_id=1, replica_groups=mesh['blk'=4,'bank'=8] {'bank'}, dimensions={0}, use_global_device_ids=true | all-gather | bytes 589824 | tf_op jit(solution)/shard_map/all_gather | solution.py:57
  118.8 0.3 fusion.37
  119.2 0.8 copy.6
  120.0 1.1 reshape.96
  121.1 0.5 fusion.10
  121.6 0.6 fusion.1
  122.2 0.3 copy.11
  122.6 0.2 fusion.7
  122.8 0.5 fusion.11
  123.3 0.6 convolution_log_fusion
  124.0 2.0 convolution_bitcast_fusion.1
  126.0 35.1 %reduce-scatter.5.cloned.1.call-done = f32[32,8,128]{2,1,0:T(8,128)} async-done(((f32[256,8,128]{2,1,0:T(8,128)}), f32[32,8,128]{2,1,0:T(8,128)}) %reduce-scatter.5.cloned.1.call-update) | async-done | bytes 131088 | tf_op jit(solution)/shard_map/reduce_scatter | solution.py:49
  161.1 0.3 copy.13
  161.5 36.4 %all-reduce.5.cloned.1.call-done = f32[32,8,128]{2,1,0:T(8,128)} async-done(((f32[32,8,128]{2,1,0:T(8,128)}), f32[32,8,128]{2,1,0:T(8,128)}) %all-reduce.5.cloned.1.call-update) | async-done | bytes 131088 | tf_op jit(solution)/shard_map/psum | solution.py:55
  197.8 1.1 divide_convert_fusion
  198.9 9.8 %all_gather.7 = bf16[256,8,128]{2,1,0:T(8,128)(2,1)S(1)} all-gather(bf16[32,8,128]{2,1,0:T(8,128)(2,1)S(1)} %divide_convert_fusion), channel_id=1, replica_groups=mesh['blk'=4,'bank'=8] {'bank'}, dimensions={0}, use_global_device_ids=true | all-gather | bytes 589824 | tf_op jit(solution)/shard_map/all_gather | solution.py:57
  208.7 1.1 fusion
  209.8 0.7 fusion.58
  (17 shorter events, 0.3 us)
Async XLA Ops:
  7.2 60.3 %reduce-scatter.3.cloned.1.call-start = ((), (), s32[]{:S(2)}) async-start(), calls=%async_computation.2 | async-start | bytes 1179648 | tf_op jit(solution)/shard_map/reduce_scatter | solution.py:49
  23.8 1.4 copy-start
  25.4 1.2 copy-start.2
  28.6 78.4 %all-reduce.3.cloned.1.call-start = ((), (), s32[]{:S(2)}) async-start(), calls=%async_computation.3 | async-start | bytes 262144 | tf_op jit(solution)/shard_map/psum | solution.py:55
  67.5 93.6 %reduce-scatter.5.cloned.1.call-start = ((), (), s32[]{:S(2)}) async-start(), calls=%async_computation.4 | async-start | bytes 1179648 | tf_op jit(solution)/shard_map/reduce_scatter | solution.py:49
  125.9 71.9 %all-reduce.5.cloned.1.call-start = ((), (), s32[]{:S(2)}) async-start(), calls=%async_computation.5 | async-start | bytes 262144 | tf_op jit(solution)/shard_map/psum | solution.py:55
  197.8 12.0 %copy-start.1 = (f32[32,8,128]{2,1,0:T(8,128)S(1)}, f32[32,8,128]{2,1,0:T(8,128)}, u32[]{:S(2)}) copy-start(f32[32,8,128]{2,1,0:T(8,128)} %all-reduce.5.cloned.1.call-done) | copy-start | bytes 393220
Sparse Core Ops, SparseCore 0:
  28.7 38.7 reduce-scatter.2
  69.8 34.4 all-reduce.2
  126.1 35.0 reduce-scatter.4
  163.4 34.4 all-reduce.4
where the time goes:
time: 218 us; the launch traced here: 217 us
  waiting for transfers between devices  110 us (50%)
  blocking collectives  60 us (28%)
  local copies, waits for them, and re-layouts  14.5 us (7%)
  between operations  13.9 us (6%)
  matrix products  9.62 us (4%)
  other arithmetic  8.52 us (4%)
    reduce_scatter x2, waiting for transfers between devices, per_device(): lax.psum_scatter(jnp.einsum('km,mrl->rkl', member_weights, blocks, precis...  73.9 us
    psum x1, blocking collectives, per_device(): counts = lax.psum(jnp.sum(onehot, axis=0), ('blk', 'bank'))  39.4 us
    psum x2, waiting for transfers between devices, per_device(): summed = lax.psum(reduced, 'blk')  36.4 us
    all_gather x2, blocking collectives, per_device(): center_all = lax.all_gather(center_slice, 'bank', axis=0, tiled=True)  20.6 us
    convert_element_type x1, local copies, waits for them, and re-layouts, kernel_tables(): kernel_pair = (kernel_line[:, None, :, None] * kernel_line[None, :, None,...  11.3 us
    convert_element_type x1, other arithmetic, kernel_tables(): kernel_pair = (kernel_line[:, None, :, None] * kernel_line[None, :, None,...  5.26 us
  transfers between devices with their start and end apart: 4, of which 3 were waited for; matrix products, arithmetic and copies ran while one was open for 0% of the time, Pallas kernels for 0%

commit v1 on v0

v1 whole, which is shorter than its diff:
```python
import functools

import jax
import jax.numpy as jnp
import ml_dtypes
import numpy as np
from jax import lax
from jax.experimental import pallas as pl
from jax.experimental.pallas import tpu as pltpu
from jax.sharding import PartitionSpec as P

G = 32
PLANE = G * G
BARS = 8
ITERS = 2
MESH = pl.DeviceIdType.MESH
F32 = jnp.float32
BF16 = jnp.bfloat16


def host_tables():
    grid_pos = np.arange(G, dtype=np.float32)
    offset = grid_pos[:, None] - grid_pos[None, :]
    line = np.exp(np.float32(-0.5) * offset * offset)
    pair = (line[:, None, :, None] * line[None, :, None, :]).reshape(PLANE, PLANE).astype(ml_dtypes.bfloat16)
    return line, pair


def kernel(
    groups, banks, members,
    density_ref, label_ref, pair_hbm, line_ref, row_ref, column_ref,
    centers_ref, potential_ref,
    pair, raised, source, lifted, smoothed, outgoing, incoming, partial, partial_in, shared, chosen, chosen_in,
    labels, label_out, count_out, count_in,
    pair_sem, label_sem, count_sem, member_send, member_recv, partial_sem, shared_send, shared_recv, chosen_send, chosen_recv,
):
    blk, bank = lax.axis_index("blk"), lax.axis_index("bank")
    rows = G * members
    chunk = rows // banks
    slabs = G // banks
    width = PLANE // groups
    kept = slabs * BARS

    def group_at(step):
        return lax.rem(blk + step, groups)

    def bank_at(step):
        return lax.rem(bank + step, banks)

    def chunk_at(index):
        return pl.ds(pl.multiple_of(index * chunk, chunk), chunk)

    def push(src, dst, send_sem, recv_sem, device):
        pltpu.make_async_remote_copy(
            src_ref=src, dst_ref=dst, send_sem=send_sem, recv_sem=recv_sem,
            device_id=device, device_id_type=MESH,
        ).start()

    def await_bytes(ref, sem):
        pltpu.make_async_copy(ref, ref, sem).wait()

    load_pair = pltpu.make_async_copy(pair_hbm, pair, pair_sem)
    load_pair.start()
    barrier = pltpu.get_barrier_semaphore()
    for step in range(1, banks):
        pl.semaphore_signal(barrier, inc=1, device_id=(blk, bank_at(step)), device_id_type=MESH)
    for step in range(1, groups):
        pl.semaphore_signal(barrier, inc=1, device_id=(group_at(step), bank), device_id_type=MESH)

    own_rows = lax.broadcasted_iota(jnp.int32, (chunk, 128), 0) % members
    own_labels = jnp.zeros((chunk, 128), F32)
    for member in range(members):
        own_labels = jnp.where(own_rows == member, label_ref[member].astype(F32), own_labels)
    label_out[...] = own_labels.astype(BF16)
    labels[chunk_at(bank), :] = own_labels.astype(BF16)

    for tile in range(groups):
        for x in range(G):
            lifted[tile, members * x:members * (x + 1), :] = density_ref[
                :, x * PLANE + tile * width:x * PLANE + (tile + 1) * width
            ].astype(F32)
    for tile in range(groups):
        risen = jnp.exp(lifted[tile])
        lifted[tile] = risen
        columns = slice(tile * width, (tile + 1) * width)
        source[:, columns] = (risen * (row_ref[...] * column_ref[:, columns])).astype(BF16)

    pl.semaphore_wait(barrier, banks - 1 + groups - 1)
    for step in range(1, banks):
        push(label_out, labels.at[chunk_at(bank), :], label_sem.at[0], label_sem.at[1], (blk, bank_at(step)))
    load_pair.wait()

    def convolve(field, tile):
        inner = jnp.dot(field, pair[tile], preferred_element_type=F32)
        return jnp.dot(line_ref[...], inner, precision=lax.Precision.HIGHEST, preferred_element_type=F32)

    pick = None
    for iteration in range(ITERS):
        last = iteration == ITERS - 1
        if iteration:
            for tile in range(groups):
                source[:, tile * width:(tile + 1) * width] = (lifted[tile] / convolve(raised[...], tile)).astype(BF16)

        for step in range(1, groups + 1):
            tile = group_at(step)
            value = jnp.log(convolve(source[...], tile))
            smoothed[tile] = value
            outgoing[iteration, tile] = value.astype(BF16)
            incoming[iteration, tile, chunk_at(bank), :] = outgoing[iteration, tile, chunk_at(bank), :]
            for hop in range(1, banks):
                peer = bank_at(hop)
                push(
                    outgoing.at[iteration, tile, chunk_at(peer), :],
                    incoming.at[iteration, tile, chunk_at(bank), :],
                    member_send.at[iteration], member_recv.at[iteration, tile], (blk, peer),
                )

        if iteration == 0:
            await_bytes(labels.at[0:rows - chunk, :], label_sem.at[1])
            row = lax.broadcasted_iota(jnp.int32, (rows, 128), 0)
            lane = lax.broadcasted_iota(jnp.int32, (rows, 128), 1)
            match = (labels[...].astype(F32) == (lane % BARS).astype(F32)) & ((row // members) % slabs == lane // BARS)
            pick_wide = jnp.where(match, 1.0, 0.0).astype(F32)
            gather_wide = jnp.transpose(pick_wide)
            pick = pick_wide.astype(BF16)[:, :kept]
            gather = gather_wide.astype(BF16)[:kept, :]
            own_count = jnp.broadcast_to(jnp.sum(gather_wide[:BARS, :], axis=1, keepdims=True), (BARS, 128))
            count_out[...] = own_count
            count_in[blk] = own_count
            for step in range(1, groups):
                push(count_out, count_in.at[blk], count_sem.at[0], count_sem.at[1], (group_at(step), bank))

        for step in range(1, groups + 1):
            tile = group_at(step)
            await_bytes(incoming.at[iteration, tile, 0:rows - chunk, :], member_recv.at[iteration, tile])
            sums = jnp.dot(gather, incoming[iteration, tile], preferred_element_type=F32)
            if step < groups:
                partial[iteration, tile] = sums
                push(
                    partial.at[iteration, tile], partial_in.at[iteration, blk],
                    partial_sem.at[iteration, 0], partial_sem.at[iteration, 1], (tile, bank),
                )
            else:
                partial_in[iteration, blk] = sums

        if iteration == 0:
            await_bytes(count_in.at[0:groups - 1], count_sem.at[1])
            counts = functools.reduce(jnp.add, [count_in[group] for group in range(groups)])
            counts = jnp.concatenate([counts[:, :1]] * slabs, axis=0)
        await_bytes(partial_in.at[iteration, 0:groups - 1], partial_sem.at[iteration, 1])
        total = functools.reduce(jnp.add, [partial_in[iteration, group] for group in range(groups)])
        shared[iteration, blk] = (total / counts).astype(BF16)
        for step in range(1, groups):
            push(
                shared.at[iteration, blk], shared.at[iteration, blk],
                shared_send.at[iteration], shared_recv.at[iteration, blk], (group_at(step), bank),
            )

        for step in range(groups):
            tile = group_at(step)
            if step:
                await_bytes(shared.at[iteration, tile], shared_recv.at[iteration, tile])
            center = shared[iteration, tile]
            chosen[iteration, tile] = jnp.dot(pick, center, preferred_element_type=F32).astype(BF16)
            chosen_in[iteration, tile, chunk_at(bank), :] = chosen[iteration, tile, chunk_at(bank), :]
            for hop in range(1, banks):
                peer = bank_at(hop)
                push(
                    chosen.at[iteration, tile, chunk_at(peer), :],
                    chosen_in.at[iteration, tile, chunk_at(bank), :],
                    chosen_send.at[iteration], chosen_recv.at[iteration, tile], (blk, peer),
                )
            if last:
                for slab in range(slabs):
                    start = pl.multiple_of(slab * PLANE + tile * width, width)
                    centers_ref[:, pl.ds(start, width)] = center[slab * BARS:(slab + 1) * BARS, :]

        for step in range(groups):
            tile = group_at(step)
            await_bytes(chosen_in.at[iteration, tile, 0:rows - chunk, :], chosen_recv.at[iteration, tile])
            value = chosen_in[iteration, tile].astype(F32) - smoothed[tile]
            if last:
                for x in range(G):
                    start = pl.multiple_of(x * PLANE + tile * width, width)
                    potential_ref[:, pl.ds(start, width)] = value[members * x:members * (x + 1), :]
            else:
                raised[:, pl.ds(pl.multiple_of(tile * width, width), width)] = jnp.exp(value).astype(BF16)

    for _ in range(banks - 1):
        await_bytes(label_out, label_sem.at[0])
    for _ in range(groups - 1):
        await_bytes(count_out, count_sem.at[0])
    for iteration in range(ITERS):
        await_bytes(outgoing.at[iteration, :, 0:rows - chunk, :], member_send.at[iteration])
        await_bytes(partial.at[iteration, 0:groups - 1], partial_sem.at[iteration, 0])
        await_bytes(shared.at[iteration, 0:groups - 1], shared_send.at[iteration])
        await_bytes(chosen.at[iteration, :, 0:rows - chunk, :], chosen_send.at[iteration])


def fused_device(groups, banks, log_density, assignment):
    members, cells = log_density.shape
    rows, chunk = G * members, G * members // banks
    width = PLANE // groups
    kept = G // banks * BARS
    line, pair = host_tables()
    tiled_pair = np.ascontiguousarray(pair.reshape(PLANE, groups, width).transpose(1, 0, 2))
    line_rows = np.kron(line, np.eye(members, dtype=np.float32))
    row_scale = (1.0 / line_rows.sum(axis=1, keepdims=True)).astype(np.float32)
    column_scale = (1.0 / pair.astype(np.float32).sum(axis=0, keepdims=True)).astype(np.float32)
    vmem = pl.BlockSpec(memory_space=pltpu.VMEM)
    dma = pltpu.SemaphoreType.DMA
    return pl.pallas_call(
        functools.partial(kernel, groups, banks, members),
        out_shape=(
            jax.ShapeDtypeStruct((BARS, cells // banks), BF16),
            jax.ShapeDtypeStruct((members, cells), F32),
        ),
        in_specs=[vmem, pl.BlockSpec(memory_space=pltpu.SMEM), pl.BlockSpec(memory_space=pl.ANY), vmem, vmem, vmem],
        out_specs=(vmem, vmem),
        scratch_shapes=[
            pltpu.VMEM((groups, PLANE, width), BF16),
            pltpu.VMEM((rows, PLANE), BF16),
            pltpu.VMEM((rows, PLANE), BF16),
            pltpu.VMEM((groups, rows, width), F32),
            pltpu.VMEM((groups, rows, width), F32),
            pltpu.VMEM((ITERS, groups, rows, width), BF16),
            pltpu.VMEM((ITERS, groups, rows, width), BF16),
            pltpu.VMEM((ITERS, groups, kept, width), F32),
            pltpu.VMEM((ITERS, groups, kept, width), F32),
            pltpu.VMEM((ITERS, groups, kept, width), BF16),
            pltpu.VMEM((ITERS, groups, rows, width), BF16),
            pltpu.VMEM((ITERS, groups, rows, width), BF16),
            pltpu.VMEM((rows, 128), BF16),
            pltpu.VMEM((chunk, 128), BF16),
            pltpu.VMEM((BARS, 128), F32),
            pltpu.VMEM((groups, BARS, 128), F32),
            dma, dma((2,)), dma((2,)),
            dma((ITERS,)), dma((ITERS, groups)),
            dma((ITERS, 2)),
            dma((ITERS,)), dma((ITERS, groups)),
            dma((ITERS,)), dma((ITERS, groups)),
        ],
        compiler_params=pltpu.CompilerParams(
            collective_id=0, has_side_effects=True, vmem_limit_bytes=40 * 1024 * 1024
        ),
    )(log_density, assignment, jnp.asarray(tiled_pair), jnp.asarray(line_rows), jnp.asarray(row_scale), jnp.asarray(column_scale))


def log_convolve(field_log, kernel_line, kernel_pair):
    member_count = field_log.shape[0]
    raised = jnp.exp(field_log).astype(BF16).reshape(member_count * G, PLANE)
    inner_sum = jnp.dot(raised, kernel_pair, preferred_element_type=F32).reshape(member_count, G, PLANE)
    outer_sum = jnp.einsum("ij,mjc->mic", kernel_line, inner_sum, precision=lax.Precision.HIGHEST)
    return jnp.log(outer_sum).reshape(member_count, G * PLANE)


def plain_device(log_density, assignment):
    line, pair = host_tables()
    kernel_line, kernel_pair = jnp.asarray(line), jnp.asarray(pair)
    member_count, cell_count = log_density.shape
    row_count = cell_count // 128
    labels = jnp.arange(BARS, dtype=jnp.int32)
    onehot = (assignment[:, None] == labels[None, :]).astype(F32)
    counts = lax.psum(jnp.sum(onehot, axis=0), ("blk", "bank"))
    potential = jnp.zeros((member_count, cell_count), F32)
    center_owned = None
    for _ in range(ITERS):
        source = log_density.astype(F32) - log_convolve(potential, kernel_line, kernel_pair)
        smoothed = log_convolve(source, kernel_line, kernel_pair)
        blocks = smoothed.reshape(member_count, row_count, 128)
        summed = jnp.einsum("mk,mrl->rkl", onehot, blocks, precision=lax.Precision.HIGHEST)
        summed = lax.psum_scatter(summed, "bank", scatter_dimension=0, tiled=True)
        summed = lax.psum(summed, "blk")
        center_owned = (summed / counts[None, :, None]).astype(BF16)
        center_all = lax.all_gather(center_owned, "bank", axis=0, tiled=True)
        chosen = jnp.einsum("mk,rkl->mrl", onehot.astype(BF16), center_all, preferred_element_type=F32)
        potential = chosen.reshape(member_count, cell_count) - smoothed
    centers = jnp.transpose(center_owned, (1, 0, 2)).reshape(BARS, center_owned.shape[0] * 128)
    return centers, potential


def solution(mesh):
    groups, banks = mesh.shape["blk"], mesh.shape["bank"]

    def per_device(log_density, assignment):
        rows = G * log_density.shape[0]
        fits = G % banks == 0 and (rows // banks) % 16 == 0 and PLANE % (128 * groups) == 0
        if fits and min(groups, banks) > 1:
            return fused_device(groups, banks, log_density, assignment)
        return plain_device(log_density, assignment)

    placed = (P(("blk", "bank"), None), P(("blk", "bank")))
    return jax.shard_map(
        per_device,
        mesh=mesh,
        in_specs=placed,
        out_specs=(P(None, "bank"), P(("blk", "bank"), None)),
        check_vma=False,
    )
```

time: 218 us -> 48.9 us (0.22)
  waiting for transfers between devices: 110 us -> 0 us
  blocking collectives: 60 us -> 0 us
  Pallas kernels: 0 us -> 41 us
  between operations: 13.9 us -> 0.65 us
  matrix products: 9.62 us -> 0 us
  other arithmetic: 8.52 us -> 0 us
  local copies, waits for them, and re-layouts: 14.5 us -> 6.98 us
    reduce_scatter x2 -> x0, waiting for transfers between devices: 73.9 us -> none  [per_device(): lax.psum_scatter(jnp.einsum('km,mrl->rkl', member_weights, blocks, precis...]
    pallas_call x0 -> x1, Pallas kernels: none -> 41 us  [fused_device(): pl.pallas_call(functools.partial(kernel, groups, banks, members), out_sha...]
    psum x1 -> x0, blocking collectives: 39.4 us -> none  [per_device(): counts = lax.psum(jnp.sum(onehot, axis=0), ('blk', 'bank'))]
    psum x2 -> x0, waiting for transfers between devices: 36.4 us -> none  [per_device(): summed = lax.psum(reduced, 'blk')]
    all_gather x2 -> x0, blocking collectives: 20.6 us -> none  [per_device(): center_all = lax.all_gather(center_slice, 'bank', axis=0, tiled=True)]
    convert_element_type x1 -> x0, local copies, waits for them, and re-layouts: 11.3 us -> none  [kernel_tables(): kernel_pair = (kernel_line[:, None, :, None] * kernel_line[None, :, None,...]
    dot_general x12 -> x0, matrix products: 9.62 us -> none  [the longest x2 3.91 us: per_device(): jnp.einsum('km,mrl->rkl', member_weights, blocks, precision=lax.Precision...]
    convert_element_type x5 -> x0, other arithmetic: 7.7 us -> none  [the longest x1 5.26 us: kernel_tables(): kernel_pair = (kernel_line[:, None, :, None] * kernel_line[None, :, None,...]
  transfers between devices with their start and end apart: 4 -> 0, of which waited for: 3 -> 0; matrix products, arithmetic and copies ran while one was open for 0% -> 0% of each run, Pallas kernels for 0% -> 0%
where the time goes in v1:
time: 48.9 us; the launch traced here: 48.6 us
  Pallas kernels  41 us (84%)
  local copies, waits for them, and re-layouts  6.98 us (14%)
  between operations  0.65 us (1%)
    pallas_call x1, Pallas kernels, fused_device(): pl.pallas_call(functools.partial(kernel, groups, banks, members), out_sha...  41 us
    unnamed x14, local copies, waits for them, and re-layouts  6.98 us

profile of v1, /device:TPU:0, one launch (start us, length us, event | category | flops | bytes accessed | tf_op | source)
XLA Modules:
  0.0 48.6 jit_solution(3316341473303581400)
XLA Ops:
  0.6 0.0 copy-start
  0.6 1.6 %copy-done = bf16[4,1024,256]{2,1,0:T(8,128)(2,1)S(1)} copy-done((bf16[4,1024,256]{2,1,0:T(8,128)(2,1)S(1)}, bf16[4,1024,256]{2,1,0:T(8,128)(2,1)}, u32[]{:S(2)}) %copy-start) | copy-done | bytes 2097176
  2.2 0.0 copy-start.1
  2.2 0.9 %copy-done.1 = bf16[4,32768]{1,0:T(4,128)(2,1)S(1)} copy-done((bf16[4,32768]{1,0:T(4,128)(2,1)S(1)}, bf16[4,32768]{1,0:T(4,128)(2,1)}, u32[]{:S(2)}) %copy-start.1) | copy-done | bytes 262168
  3.2 0.0 copy-start.2
  3.2 0.8 %copy-done.2 = f32[128,1]{1,0:T(8,128)S(1)} copy-done((f32[128,1]{1,0:T(8,128)S(1)}, f32[128,1]{1,0:T(8,128)}, u32[]{:S(2)}) %copy-start.2) | copy-done | bytes 536
  4.0 0.0 copy-start.3
  4.0 0.8 %copy-done.3 = f32[128,128]{1,0:T(8,128)S(1)} copy-done((f32[128,128]{1,0:T(8,128)S(1)}, f32[128,128]{1,0:T(8,128)}, u32[]{:S(2)}) %copy-start.3) | copy-done | bytes 65560
  4.9 0.0 copy-start.4
  4.9 0.7 %copy-done.4 = f32[1,1024]{1,0:T(1,128)S(1)} copy-done((f32[1,1024]{1,0:T(1,128)S(1)}, f32[1,1024]{1,0:T(1,128)}, u32[]{:S(2)}) %copy-start.4) | copy-done | bytes 4120
  5.5 0.0 copy-start.5
  5.5 0.7 %copy-done.5 = s32[4]{0:T(128)S(1)} copy-done((s32[4]{0:T(128)S(1)}, s32[4]{0:T(128)}, u32[]{:S(2)}) %copy-start.5) | copy-done | bytes 40
  6.2 41.0 %shard_map.77 = (bf16[8,4096]{1,0:T(8,128)(2,1)S(1)}, f32[4,32768]{1,0:T(4,128)S(1)}) custom-call(bf16[4,32768]{1,0:T(4,128)(2,1)S(1)} %copy-done.1, s32[4]{0:T(128)S(1)} %copy-done.5, bf16[4,1024,256]{2,1,0:T(8,128)(2,1)S(1)} %copy-done, f32[128,128]{1,0:T(8,128)S(1)} %copy-done.3, f32[128,1]{1,0:T(8,128)S(1)} %copy-done.2, f32[1,1024]{1,0:T(1,128)S(1)} %copy-done.4), custom_call_target="tpu_custom_call" | custom-call | tf_op jit(solution)/shard_map/pallas_call | solution.py:212
  47.2 0.6 %copy.10 = bf16[8,4096]{1,0:T(8,128)(2,1)} copy(bf16[8,4096]{1,0:T(8,128)(2,1)S(1)} %get-tuple-element.4) | data formatting | bytes 131072
  47.8 0.8 %copy.11 = f32[4,32768]{1,0:T(4,128)} copy(f32[4,32768]{1,0:T(4,128)S(1)} %get-tuple-element.5) | data formatting | bytes 1048576
Async XLA Ops:
  0.6 1.6 %copy-start = (bf16[4,1024,256]{2,1,0:T(8,128)(2,1)S(1)}, bf16[4,1024,256]{2,1,0:T(8,128)(2,1)}, u32[]{:S(2)}) copy-start(bf16[4,1024,256]{2,1,0:T(8,128)(2,1)} %constant.8.clone.pair_hbm) | copy-start | bytes 6291460
  2.2 0.9 %copy-start.1 = (bf16[4,32768]{1,0:T(4,128)(2,1)S(1)}, bf16[4,32768]{1,0:T(4,128)(2,1)}, u32[]{:S(2)}) copy-start(bf16[4,32768]{1,0:T(4,128)(2,1)} %density_ref.1) | copy-start | bytes 786436
  3.2 0.8 %copy-start.2 = (f32[128,1]{1,0:T(8,128)S(1)}, f32[128,1]{1,0:T(8,128)}, u32[]{:S(2)}) copy-start(f32[128,1]{1,0:T(8,128)} %constant.10.clone.row_ref) | copy-start | bytes 1540
  4.0 0.8 %copy-start.3 = (f32[128,128]{1,0:T(8,128)S(1)}, f32[128,128]{1,0:T(8,128)}, u32[]{:S(2)}) copy-start(f32[128,128]{1,0:T(8,128)} %constant.9.clone.line_ref) | copy-start | bytes 196612
  4.9 0.7 %copy-start.4 = (f32[1,1024]{1,0:T(1,128)S(1)}, f32[1,1024]{1,0:T(1,128)}, u32[]{:S(2)}) copy-start(f32[1,1024]{1,0:T(1,128)} %constant.11.clone.column_ref) | copy-start | bytes 12292
  5.5 0.7 %copy-start.5 = (s32[4]{0:T(128)S(1)}, s32[4]{0:T(128)}, u32[]{:S(2)}) copy-start(s32[4]{0:T(128)} %label_ref.1) | copy-start | bytes 52

commit v2 on v1

v2 whole, which is shorter than its diff:
```python
import functools

import jax
import jax.numpy as jnp
import ml_dtypes
import numpy as np
from jax import lax
from jax.experimental import pallas as pl
from jax.experimental.pallas import tpu as pltpu
from jax.sharding import PartitionSpec as P

G = 32
PLANE = G * G
BARS = 8
ITERS = 2
SENDS = 1
RETURNS = 1
MESH = pl.DeviceIdType.MESH
F32 = jnp.float32
BF16 = jnp.bfloat16


def host_tables():
    grid_pos = np.arange(G, dtype=np.float32)
    offset = grid_pos[:, None] - grid_pos[None, :]
    line = np.exp(np.float32(-0.5) * offset * offset)
    pair = (line[:, None, :, None] * line[None, :, None, :]).reshape(PLANE, PLANE).astype(ml_dtypes.bfloat16)
    return line, pair


def kernel(
    groups, banks, members,
    density_hbm, label_hbm, pair_hbm, line_hbm, scale_hbm,
    centers_ref, potential_ref,
    density_ref, label_ref, line_ref, scale_ref, pair, raised, source, lifted, smoothed, outgoing, incoming, partial, partial_in, shared, chosen, chosen_in,
    labels, label_out, count_out, count_in,
    load_sem, label_sem, count_sem, member_send, member_recv, partial_sem, shared_send, shared_recv, chosen_send, chosen_recv,
):
    blk, bank = lax.axis_index("blk"), lax.axis_index("bank")
    rows = G * members
    chunk = rows // banks
    slabs = G // banks
    width = PLANE // groups
    kept = slabs * BARS

    def group_at(step):
        return lax.rem(blk + step, groups)

    def bank_at(step):
        return lax.rem(bank + step, banks)

    def chunk_at(index):
        return pl.ds(pl.multiple_of(index * chunk, chunk), chunk)

    def part_at(step, parts):
        return lax.rem(blk // (groups // parts) + step, parts) * (groups // parts)

    def spread(src, dst, iteration, first, parts, send_sem, recv_sem):
        size = groups // parts
        for offset in range(size):
            dst[iteration, first + offset, chunk_at(bank), :] = src[iteration, first + offset, chunk_at(bank), :]
        for hop in range(1, banks):
            peer = bank_at(hop)
            push(
                src.at[iteration, pl.ds(first, size), chunk_at(peer), :],
                dst.at[iteration, pl.ds(first, size), chunk_at(bank), :],
                send_sem.at[iteration], recv_sem.at[iteration, first // size], (blk, peer),
            )

    def await_spread(dst, iteration, first, parts, recv_sem):
        size = groups // parts
        await_bytes(dst.at[iteration, pl.ds(first, size), 0:rows - chunk, :], recv_sem.at[iteration, first // size])

    def push(src, dst, send_sem, recv_sem, device):
        pltpu.make_async_remote_copy(
            src_ref=src, dst_ref=dst, send_sem=send_sem, recv_sem=recv_sem,
            device_id=device, device_id_type=MESH,
        ).start()

    def await_bytes(ref, sem):
        pltpu.make_async_copy(ref, ref, sem).wait()

    loads = [
        pltpu.make_async_copy(src, dst, load_sem.at[index])
        for index, (src, dst) in enumerate((
            (density_hbm, density_ref), (label_hbm, label_ref), (scale_hbm, scale_ref),
            (line_hbm, line_ref), (pair_hbm, pair),
        ))
    ]
    for load in loads:
        load.start()
    barrier = pltpu.get_barrier_semaphore()
    for step in range(1, banks):
        pl.semaphore_signal(barrier, inc=1, device_id=(blk, bank_at(step)), device_id_type=MESH)
    for step in range(1, groups):
        pl.semaphore_signal(barrier, inc=1, device_id=(group_at(step), bank), device_id_type=MESH)

    loads[1].wait()
    own_rows = lax.broadcasted_iota(jnp.int32, (chunk, 128), 0) % members
    own_labels = jnp.zeros((chunk, 128), F32)
    for member in range(members):
        own_labels = jnp.where(own_rows == member, label_ref[member].astype(F32), own_labels)
    label_out[...] = own_labels.astype(BF16)
    labels[chunk_at(bank), :] = own_labels.astype(BF16)

    loads[0].wait()
    for tile in range(groups):
        for x in range(G):
            lifted[tile, members * x:members * (x + 1), :] = density_ref[
                :, x * PLANE + tile * width:x * PLANE + (tile + 1) * width
            ].astype(F32)
    loads[2].wait()
    for tile in range(groups):
        risen = jnp.exp(lifted[tile])
        lifted[tile] = risen
        for part in range(width // 128):
            column = tile * (width // 128) + part
            scale = scale_ref[:rows, :] * scale_ref[rows + column:rows + column + 1, :]
            source[:, column * 128:(column + 1) * 128] = (risen[:, part * 128:(part + 1) * 128] * scale).astype(BF16)
    loads[3].wait()
    loads[4].wait()

    def convolve(field, tile):
        inner = jnp.dot(field, pair[tile], preferred_element_type=F32)
        high = inner.astype(BF16)
        low = (inner - high.astype(F32)).astype(BF16)
        return jnp.dot(line_ref[...], jnp.concatenate([high, high, low], axis=0), preferred_element_type=F32)

    pick = None
    for iteration in range(ITERS):
        last = iteration == ITERS - 1
        if iteration:
            for tile in range(groups):
                source[:, tile * width:(tile + 1) * width] = (lifted[tile] / convolve(raised[...], tile)).astype(BF16)

        for step in range(1, SENDS + 1):
            first = part_at(step, SENDS)
            for offset in range(groups // SENDS):
                tile = first + offset
                value = jnp.log(convolve(source[...], tile))
                smoothed[tile] = value
                outgoing[iteration, tile] = value.astype(BF16)
            if iteration == 0 and step == 1:
                pl.semaphore_wait(barrier, banks - 1 + groups - 1)
                for hop in range(1, banks):
                    push(label_out, labels.at[chunk_at(bank), :], label_sem.at[0], label_sem.at[1], (blk, bank_at(hop)))
            spread(outgoing, incoming, iteration, first, SENDS, member_send, member_recv)

        if iteration == 0:
            await_bytes(labels.at[0:rows - chunk, :], label_sem.at[1])
            row = lax.broadcasted_iota(jnp.int32, (rows, 128), 0)
            lane = lax.broadcasted_iota(jnp.int32, (rows, 128), 1)
            match = (labels[...].astype(F32) == (lane % BARS).astype(F32)) & ((row // members) % slabs == lane // BARS)
            pick_wide = jnp.where(match, 1.0, 0.0).astype(F32)
            gather_wide = jnp.transpose(pick_wide)
            pick = pick_wide.astype(BF16)[:, :kept]
            gather = gather_wide.astype(BF16)[:kept, :]
            own_count = jnp.broadcast_to(jnp.sum(gather_wide[:BARS, :], axis=1, keepdims=True), (BARS, 128))
            count_out[...] = own_count
            count_in[blk] = own_count
            for step in range(1, groups):
                push(count_out, count_in.at[blk], count_sem.at[0], count_sem.at[1], (group_at(step), bank))

        for step in range(1, SENDS + 1):
            first = part_at(step, SENDS)
            await_spread(incoming, iteration, first, SENDS, member_recv)
            for offset in range(groups // SENDS):
                tile = first + offset
                sums = jnp.dot(gather, incoming[iteration, tile], preferred_element_type=F32)
                partial[iteration, tile] = sums.astype(BF16)

                @pl.when(tile != blk)
                def _():
                    push(
                        partial.at[iteration, tile], partial_in.at[iteration, blk],
                        partial_sem.at[iteration, 0], partial_sem.at[iteration, 1], (tile, bank),
                    )
        partial_in[iteration, blk] = partial[iteration, blk]

        if iteration == 0:
            await_bytes(count_in.at[0:groups - 1], count_sem.at[1])
            counts = functools.reduce(jnp.add, [count_in[group] for group in range(groups)])
            counts = jnp.concatenate([counts[:, :1]] * slabs, axis=0)
        await_bytes(partial_in.at[iteration, 0:groups - 1], partial_sem.at[iteration, 1])
        total = functools.reduce(jnp.add, [partial_in[iteration, group].astype(F32) for group in range(groups)])
        shared[iteration, blk] = (total / counts).astype(BF16)
        for step in range(1, groups):
            push(
                shared.at[iteration, blk], shared.at[iteration, blk],
                shared_send.at[iteration], shared_recv.at[iteration, blk], (group_at(step), bank),
            )

        for step in range(RETURNS):
            first = part_at(step, RETURNS)
            for offset in range(groups // RETURNS):
                tile = first + offset

                @pl.when(tile != blk)
                def _():
                    await_bytes(shared.at[iteration, tile], shared_recv.at[iteration, tile])

                center = shared[iteration, tile]
                chosen[iteration, tile] = jnp.dot(pick, center, preferred_element_type=F32).astype(BF16)
            spread(chosen, chosen_in, iteration, first, RETURNS, chosen_send, chosen_recv)
            if last:
                for offset in range(groups // RETURNS):
                    tile = first + offset
                    for slab in range(slabs):
                        start = pl.multiple_of(slab * PLANE + tile * width, width)
                        centers_ref[:, pl.ds(start, width)] = shared[iteration, tile, slab * BARS:(slab + 1) * BARS, :]

        for step in range(RETURNS):
            first = part_at(step, RETURNS)
            await_spread(chosen_in, iteration, first, RETURNS, chosen_recv)
            for offset in range(groups // RETURNS):
                tile = first + offset
                value = chosen_in[iteration, tile].astype(F32) - smoothed[tile]
                if last:
                    for x in range(G):
                        start = pl.multiple_of(x * PLANE + tile * width, width)
                        potential_ref[:, pl.ds(start, width)] = value[members * x:members * (x + 1), :]
                else:
                    raised[:, pl.ds(pl.multiple_of(tile * width, width), width)] = jnp.exp(value).astype(BF16)

    for _ in range(banks - 1):
        await_bytes(label_out, label_sem.at[0])
    for _ in range(groups - 1):
        await_bytes(count_out, count_sem.at[0])
    for iteration in range(ITERS):
        await_bytes(outgoing.at[iteration, :, 0:rows - chunk, :], member_send.at[iteration])
        await_bytes(partial.at[iteration, 0:groups - 1], partial_sem.at[iteration, 0])
        await_bytes(shared.at[iteration, 0:groups - 1], shared_send.at[iteration])
        await_bytes(chosen.at[iteration, :, 0:rows - chunk, :], chosen_send.at[iteration])


def fused_device(groups, banks, log_density, assignment):
    members, cells = log_density.shape
    rows, chunk = G * members, G * members // banks
    width = PLANE // groups
    kept = G // banks * BARS
    line, pair = host_tables()
    tiled_pair = np.ascontiguousarray(pair.reshape(PLANE, groups, width).transpose(1, 0, 2))
    line_rows = np.kron(line, np.eye(members, dtype=np.float32))
    high = line_rows.astype(ml_dtypes.bfloat16)
    low = (line_rows - high.astype(np.float32)).astype(ml_dtypes.bfloat16)
    line_parts = np.concatenate([high, low, high], axis=1)
    row_scale = np.broadcast_to(1.0 / line_rows.sum(axis=1, keepdims=True), (rows, 128))
    column_scale = (1.0 / pair.astype(np.float32).sum(axis=0)).reshape(PLANE // 128, 128)
    scales = np.concatenate([row_scale, column_scale], axis=0).astype(np.float32)
    vmem = pl.BlockSpec(memory_space=pltpu.VMEM)
    dma = pltpu.SemaphoreType.DMA
    return pl.pallas_call(
        functools.partial(kernel, groups, banks, members),
        out_shape=(
            jax.ShapeDtypeStruct((BARS, cells // banks), BF16),
            jax.ShapeDtypeStruct((members, cells), F32),
        ),
        in_specs=[pl.BlockSpec(memory_space=pltpu.HBM)] * 5,
        out_specs=(vmem, vmem),
        scratch_shapes=[
            pltpu.VMEM(log_density.shape, BF16),
            pltpu.SMEM(assignment.shape, jnp.int32),
            pltpu.VMEM(line_parts.shape, BF16),
            pltpu.VMEM(scales.shape, F32),
            pltpu.VMEM((groups, PLANE, width), BF16),
            pltpu.VMEM((rows, PLANE), BF16),
            pltpu.VMEM((rows, PLANE), BF16),
            pltpu.VMEM((groups, rows, width), F32),
            pltpu.VMEM((groups, rows, width), F32),
            pltpu.VMEM((ITERS, groups, rows, width), BF16),
            pltpu.VMEM((ITERS, groups, rows, width), BF16),
            pltpu.VMEM((ITERS, groups, kept, width), BF16),
            pltpu.VMEM((ITERS, groups, kept, width), BF16),
            pltpu.VMEM((ITERS, groups, kept, width), BF16),
            pltpu.VMEM((ITERS, groups, rows, width), BF16),
            pltpu.VMEM((ITERS, groups, rows, width), BF16),
            pltpu.VMEM((rows, 128), BF16),
            pltpu.VMEM((chunk, 128), BF16),
            pltpu.VMEM((BARS, 128), F32),
            pltpu.VMEM((groups, BARS, 128), F32),
            dma((5,)), dma((2,)), dma((2,)),
            dma((ITERS,)), dma((ITERS, groups)),
            dma((ITERS, 2)),
            dma((ITERS,)), dma((ITERS, groups)),
            dma((ITERS,)), dma((ITERS, groups)),
        ],
        compiler_params=pltpu.CompilerParams(
            collective_id=0, has_side_effects=True, vmem_limit_bytes=64 * 1024 * 1024 - 640 * 1024
        ),
    )(log_density, assignment, jnp.asarray(tiled_pair), jnp.asarray(line_parts), jnp.asarray(scales))


def log_convolve(field_log, kernel_line, kernel_pair):
    member_count = field_log.shape[0]
    raised = jnp.exp(field_log).astype(BF16).reshape(member_count * G, PLANE)
    inner_sum = jnp.dot(raised, kernel_pair, preferred_element_type=F32).reshape(member_count, G, PLANE)
    outer_sum = jnp.einsum("ij,mjc->mic", kernel_line, inner_sum, precision=lax.Precision.HIGHEST)
    return jnp.log(outer_sum).reshape(member_count, G * PLANE)


def plain_device(log_density, assignment):
    line, pair = host_tables()
    kernel_line, kernel_pair = jnp.asarray(line), jnp.asarray(pair)
    member_count, cell_count = log_density.shape
    row_count = cell_count // 128
    labels = jnp.arange(BARS, dtype=jnp.int32)
    onehot = (assignment[:, None] == labels[None, :]).astype(F32)
    counts = lax.psum(jnp.sum(onehot, axis=0), ("blk", "bank"))
    potential = jnp.zeros((member_count, cell_count), F32)
    center_owned = None
    for _ in range(ITERS):
        source = log_density.astype(F32) - log_convolve(potential, kernel_line, kernel_pair)
        smoothed = log_convolve(source, kernel_line, kernel_pair)
        blocks = smoothed.reshape(member_count, row_count, 128)
        summed = jnp.einsum("mk,mrl->rkl", onehot, blocks, precision=lax.Precision.HIGHEST)
        summed = lax.psum_scatter(summed, "bank", scatter_dimension=0, tiled=True)
        summed = lax.psum(summed, "blk")
        center_owned = (summed / counts[None, :, None]).astype(BF16)
        center_all = lax.all_gather(center_owned, "bank", axis=0, tiled=True)
        chosen = jnp.einsum("mk,rkl->mrl", onehot.astype(BF16), center_all, preferred_element_type=F32)
        potential = chosen.reshape(member_count, cell_count) - smoothed
    centers = jnp.transpose(center_owned, (1, 0, 2)).reshape(BARS, center_owned.shape[0] * 128)
    return centers, potential


def solution(mesh):
    groups, banks = mesh.shape["blk"], mesh.shape["bank"]

    def per_device(log_density, assignment):
        rows = G * log_density.shape[0]
        fits = G % banks == 0 and (rows // banks) % 16 == 0 and PLANE % (128 * groups) == 0
        if fits and min(groups, banks) > 1:
            return fused_device(groups, banks, log_density, assignment)
        return plain_device(log_density, assignment)

    placed = (P(("blk", "bank"), None), P(("blk", "bank")))
    return jax.shard_map(
        per_device,
        mesh=mesh,
        in_specs=placed,
        out_specs=(P(None, "bank"), P(("blk", "bank"), None)),
        check_vma=False,
    )
```

time: 48.9 us -> 47.7 us (0.975)
  local copies, waits for them, and re-layouts: 6.98 us -> 3.34 us
  Pallas kernels: 41 us -> 43.5 us
    unnamed x14 -> x2, local copies, waits for them, and re-layouts: 6.98 us -> 3.34 us
    pallas_call x1, Pallas kernels: 41 us -> 43.5 us  [fused_device(): pl.pallas_call(functools.partial(kernel, groups, banks, members), out_sha...]
where the time goes in v2:
time: 47.7 us; the launch traced here: 47.4 us
  Pallas kernels  43.5 us (91%)
  local copies, waits for them, and re-layouts  3.34 us (7%)
  between operations  0.64 us (1%)
    pallas_call x1, Pallas kernels, fused_device(): pl.pallas_call(functools.partial(kernel, groups, banks, members), out_sha...  43.5 us
    unnamed x2, local copies, waits for them, and re-layouts  3.34 us

profile of v2, /device:TPU:0, one launch (start us, length us, event | category | flops | bytes accessed | tf_op | source)
XLA Modules:
  0.0 47.4 jit_solution(13540972701748977700)
XLA Ops:
  0.6 43.5 %shard_map.68 = (bf16[8,4096]{1,0:T(8,128)(2,1)}, f32[4,32768]{1,0:T(4,128)}) custom-call(bf16[4,32768]{1,0:T(4,128)(2,1)} %density_hbm.1, s32[4]{0:T(128)} %label_hbm.1, bf16[4,1024,256]{2,1,0:T(8,128)(2,1)} %constant.6.clone.pair_hbm, bf16[128,384]{1,0:T(8,128)(2,1)} %constant.7.clone.line_hbm, f32[136,128]{1,0:T(8,128)} %constant.8.clone.scale_hbm), custom_call_target="tpu_custom_call" | custom-call | tf_op jit(solution)/shard_map/pallas_call | solution.py:252
  44.1 1.5 %copy.9 = bf16[8,4096]{1,0:T(8,128)(2,1)} copy(bf16[8,4096]{1,0:T(8,128)(2,1)} %get-tuple-element.4) | data formatting | bytes 131072
  45.6 1.9 %copy.10 = f32[4,32768]{1,0:T(4,128)} copy(f32[4,32768]{1,0:T(4,128)} %get-tuple-element.5) | data formatting | bytes 1048576

commit v3 on v1

--- a/solution.py
+++ b/solution.py
@@ -28,11 +28,11 @@
 
 def kernel(
     groups, banks, members,
-    density_ref, label_ref, pair_hbm, line_ref, row_ref, column_ref,
+    density_hbm, label_hbm, pair_hbm, line_hbm, scale_hbm,
     centers_ref, potential_ref,
-    pair, raised, source, lifted, smoothed, outgoing, incoming, partial, partial_in, shared, chosen, chosen_in,
+    density_ref, label_ref, line_ref, scale_ref, pair, raised, source, lifted, smoothed, outgoing, incoming, partial, partial_in, shared, chosen, chosen_in,
     labels, label_out, count_out, count_in,
-    pair_sem, label_sem, count_sem, member_send, member_recv, partial_sem, shared_send, shared_recv, chosen_send, chosen_recv,
+    load_sem, label_sem, count_sem, member_send, member_recv, partial_sem, shared_send, shared_recv, chosen_send, chosen_recv,
 ):
     blk, bank = lax.axis_index("blk"), lax.axis_index("bank")
     rows = G * members
@@ -50,6 +50,25 @@
     def chunk_at(index):
         return pl.ds(pl.multiple_of(index * chunk, chunk), chunk)
 
+    def tile_at(step):
+        if step == groups - 1:
+            return blk
+        up = step + (blk <= step).astype(jnp.int32)
+        down = groups - 1 - step - (groups - 1 - blk <= step).astype(jnp.int32)
+        return jnp.where(2 * blk >= groups, up, down)
+
+    def spread(src, dst, iteration, tile, send_sem, recv_sem):
+        for hop in range(1, banks):
+            peer = bank_at(hop)
+            push(
+                src.at[iteration, tile, chunk_at(peer), :], dst.at[iteration, tile, chunk_at(bank), :],
+                send_sem.at[iteration], recv_sem.at[iteration, tile], (blk, peer),
+            )
+        dst[iteration, tile, chunk_at(bank), :] = src[iteration, tile, chunk_at(bank), :]
+
+    def await_spread(dst, iteration, tile, recv_sem):
+        await_bytes(dst.at[iteration, tile, 0:rows - chunk, :], recv_sem.at[iteration, tile])
+
     def push(src, dst, send_sem, recv_sem, device):
         pltpu.make_async_remote_copy(
             src_ref=src, dst_ref=dst, send_sem=send_sem, recv_sem=recv_sem,
@@ -59,14 +78,22 @@
     def await_bytes(ref, sem):
         pltpu.make_async_copy(ref, ref, sem).wait()
 
-    load_pair = pltpu.make_async_copy(pair_hbm, pair, pair_sem)
-    load_pair.start()
+    loads = [
+        pltpu.make_async_copy(src, dst, load_sem.at[index])
+        for index, (src, dst) in enumerate((
+            (density_hbm, density_ref), (label_hbm, label_ref), (scale_hbm, scale_ref),
+            (line_hbm, line_ref), (pair_hbm, pair),
+        ))
+    ]
+    for load in loads:
+        load.start()
     barrier = pltpu.get_barrier_semaphore()
     for step in range(1, banks):
         pl.semaphore_signal(barrier, inc=1, device_id=(blk, bank_at(step)), device_id_type=MESH)
     for step in range(1, groups):
         pl.semaphore_signal(barrier, inc=1, device_id=(group_at(step), bank), device_id_type=MESH)
 
+    loads[1].wait()
     own_rows = lax.broadcasted_iota(jnp.int32, (chunk, 128), 0) % members
     own_labels = jnp.zeros((chunk, 128), F32)
     for member in range(members):
@@ -74,25 +101,28 @@
     label_out[...] = own_labels.astype(BF16)
     labels[chunk_at(bank), :] = own_labels.astype(BF16)
 
+    loads[0].wait()
     for tile in range(groups):
         for x in range(G):
             lifted[tile, members * x:members * (x + 1), :] = density_ref[
                 :, x * PLANE + tile * width:x * PLANE + (tile + 1) * width
             ].astype(F32)
+    loads[2].wait()
     for tile in range(groups):
         risen = jnp.exp(lifted[tile])
         lifted[tile] = risen
-        columns = slice(tile * width, (tile + 1) * width)
-        source[:, columns] = (risen * (row_ref[...] * column_ref[:, columns])).astype(BF16)
-
-    pl.semaphore_wait(barrier, banks - 1 + groups - 1)
-    for step in range(1, banks):
-        push(label_out, labels.at[chunk_at(bank), :], label_sem.at[0], label_sem.at[1], (blk, bank_at(step)))
-    load_pair.wait()
+        for part in range(width // 128):
+            column = tile * (width // 128) + part
+            scale = scale_ref[:rows, :] * scale_ref[rows + column:rows + column + 1, :]
+            source[:, column * 128:(column + 1) * 128] = (risen[:, part * 128:(part + 1) * 128] * scale).astype(BF16)
+    loads[3].wait()
+    loads[4].wait()
 
     def convolve(field, tile):
         inner = jnp.dot(field, pair[tile], preferred_element_type=F32)
-        return jnp.dot(line_ref[...], inner, precision=lax.Precision.HIGHEST, preferred_element_type=F32)
+        high = inner.astype(BF16)
+        low = (inner - high.astype(F32)).astype(BF16)
+        return jnp.dot(line_ref[...], jnp.concatenate([high, high, low], axis=0), preferred_element_type=F32)
 
     pick = None
     for iteration in range(ITERS):
@@ -101,19 +131,16 @@
             for tile in range(groups):
                 source[:, tile * width:(tile + 1) * width] = (lifted[tile] / convolve(raised[...], tile)).astype(BF16)
 
-        for step in range(1, groups + 1):
-            tile = group_at(step)
+        for step in range(groups):
+            tile = tile_at(step)
             value = jnp.log(convolve(source[...], tile))
             smoothed[tile] = value
             outgoing[iteration, tile] = value.astype(BF16)
-            incoming[iteration, tile, chunk_at(bank), :] = outgoing[iteration, tile, chunk_at(bank), :]
-            for hop in range(1, banks):
-                peer = bank_at(hop)
-                push(
-                    outgoing.at[iteration, tile, chunk_at(peer), :],
-                    incoming.at[iteration, tile, chunk_at(bank), :],
-                    member_send.at[iteration], member_recv.at[iteration, tile], (blk, peer),
-                )
+            if iteration == 0 and step == 0:
+                pl.semaphore_wait(barrier, banks - 1 + groups - 1)
+                for hop in range(1, banks):
+                    push(label_out, labels.at[chunk_at(bank), :], label_sem.at[0], label_sem.at[1], (blk, bank_at(hop)))
+            spread(outgoing, incoming, iteration, tile, member_send, member_recv)
 
         if iteration == 0:
             await_bytes(labels.at[0:rows - chunk, :], label_sem.at[1])
@@ -130,11 +157,11 @@
             for step in range(1, groups):
                 push(count_out, count_in.at[blk], count_sem.at[0], count_sem.at[1], (group_at(step), bank))
 
-        for step in range(1, groups + 1):
-            tile = group_at(step)
-            await_bytes(incoming.at[iteration, tile, 0:rows - chunk, :], member_recv.at[iteration, tile])
+        for step in range(groups):
+            tile = tile_at(step)
+            await_spread(incoming, iteration, tile, member_recv)
             sums = jnp.dot(gather, incoming[iteration, tile], preferred_element_type=F32)
-            if step < groups:
+            if step < groups - 1:
                 partial[iteration, tile] = sums
                 push(
                     partial.at[iteration, tile], partial_in.at[iteration, blk],
@@ -150,34 +177,27 @@
         await_bytes(partial_in.at[iteration, 0:groups - 1], partial_sem.at[iteration, 1])
         total = functools.reduce(jnp.add, [partial_in[iteration, group] for group in range(groups)])
         shared[iteration, blk] = (total / counts).astype(BF16)
-        for step in range(1, groups):
+        for step in range(groups - 1):
             push(
                 shared.at[iteration, blk], shared.at[iteration, blk],
-                shared_send.at[iteration], shared_recv.at[iteration, blk], (group_at(step), bank),
+                shared_send.at[iteration], shared_recv.at[iteration, blk], (tile_at(step), bank),
             )
 
-        for step in range(groups):
-            tile = group_at(step)
-            if step:
+        for step in reversed(range(groups)):
+            tile = tile_at(step)
+            if step < groups - 1:
                 await_bytes(shared.at[iteration, tile], shared_recv.at[iteration, tile])
             center = shared[iteration, tile]
             chosen[iteration, tile] = jnp.dot(pick, center, preferred_element_type=F32).astype(BF16)
-            chosen_in[iteration, tile, chunk_at(bank), :] = chosen[iteration, tile, chunk_at(bank), :]
-            for hop in range(1, banks):
-                peer = bank_at(hop)
-                push(
-                    chosen.at[iteration, tile, chunk_at(peer), :],
-                    chosen_in.at[iteration, tile, chunk_at(bank), :],
-                    chosen_send.at[iteration], chosen_recv.at[iteration, tile], (blk, peer),
-                )
+            spread(chosen, chosen_in, iteration, tile, chosen_send, chosen_recv)
             if last:
                 for slab in range(slabs):
                     start = pl.multiple_of(slab * PLANE + tile * width, width)
                     centers_ref[:, pl.ds(start, width)] = center[slab * BARS:(slab + 1) * BARS, :]
 
-        for step in range(groups):
-            tile = group_at(step)
-            await_bytes(chosen_in.at[iteration, tile, 0:rows - chunk, :], chosen_recv.at[iteration, tile])
+        for step in reversed(range(groups)):
+            tile = tile_at(step)
+            await_spread(chosen_in, iteration, tile, chosen_recv)
             value = chosen_in[iteration, tile].astype(F32) - smoothed[tile]
             if last:
                 for x in range(G):
@@ -205,8 +225,13 @@
     line, pair = host_tables()
     tiled_pair = np.ascontiguousarray(pair.reshape(PLANE, groups, width).transpose(1, 0, 2))
     line_rows = np.kron(line, np.eye(members, dtype=np.float32))
-    row_scale = (1.0 / line_rows.sum(axis=1, keepdims=True)).astype(np.float32)
-    column_scale = (1.0 / pair.astype(np.float32).sum(axis=0, keepdims=True)).astype(np.float32)
+    high = line_rows.astype(ml_dtypes.bfloat16)
+    low = (line_rows - high.astype(np.float32)).astype(ml_dtypes.bfloat16)
+    line_parts = np.concatenate([high, low, high], axis=1)
+    row_scale = np.broadcast_to(1.0 / line_rows.sum(axis=1, keepdims=True), (rows, 128))
+    column_scale = (1.0 / pair.astype(np.float32).sum(axis=0)).reshape(PLANE // 128, 128)
+    scales = np.concatenate([row_scale, column_scale], axis=0).astype(np.float32)
+    operands = (log_density, assignment, jnp.asarray(tiled_pair), jnp.asarray(line_parts), jnp.asarray(scales))
     vmem = pl.BlockSpec(memory_space=pltpu.VMEM)
     dma = pltpu.SemaphoreType.DMA
     return pl.pallas_call(
@@ -215,9 +240,13 @@
             jax.ShapeDtypeStruct((BARS, cells // banks), BF16),
             jax.ShapeDtypeStruct((members, cells), F32),
         ),
-        in_specs=[vmem, pl.BlockSpec(memory_space=pltpu.SMEM), pl.BlockSpec(memory_space=pl.ANY), vmem, vmem, vmem],
+        in_specs=[pl.BlockSpec(memory_space=pltpu.HBM)] * 5,
         out_specs=(vmem, vmem),
         scratch_shapes=[
+            pltpu.VMEM(log_density.shape, BF16),
+            pltpu.SMEM(assignment.shape, jnp.int32),
+            pltpu.VMEM(line_parts.shape, BF16),
+            pltpu.VMEM(scales.shape, F32),
             pltpu.VMEM((groups, PLANE, width), BF16),
             pltpu.VMEM((rows, PLANE), BF16),
             pltpu.VMEM((rows, PLANE), BF16),
@@ -234,7 +263,7 @@
             pltpu.VMEM((chunk, 128), BF16),
             pltpu.VMEM((BARS, 128), F32),
             pltpu.VMEM((groups, BARS, 128), F32),
-            dma, dma((2,)), dma((2,)),
+            dma((5,)), dma((2,)), dma((2,)),
             dma((ITERS,)), dma((ITERS, groups)),
             dma((ITERS, 2)),
             dma((ITERS,)), dma((ITERS, groups)),
@@ -243,7 +272,7 @@
         compiler_params=pltpu.CompilerParams(
             collective_id=0, has_side_effects=True, vmem_limit_bytes=40 * 1024 * 1024
         ),
-    )(log_density, assignment, jnp.asarray(tiled_pair), jnp.asarray(line_rows), jnp.asarray(row_scale), jnp.asarray(column_scale))
+    )(*(pltpu.with_memory_space_constraint(operand, pltpu.HBM) for operand in operands))
 
 
 def log_convolve(field_log, kernel_line, kernel_pair):

time: 48.9 us -> 41 us (0.84)
  local copies, waits for them, and re-layouts: 6.98 us -> 1.42 us
  Pallas kernels: 41 us -> 38.8 us
    unnamed x14 -> x2, local copies, waits for them, and re-layouts: 6.98 us -> 1.42 us
    pallas_call x1, Pallas kernels: 41 us -> 38.8 us  [fused_device(): pl.pallas_call(functools.partial(kernel, groups, banks, members), out_sha...]
where the time goes in v3:
time: 41 us; the launch traced here: 40.9 us
  Pallas kernels  38.8 us (95%)
  local copies, waits for them, and re-layouts  1.42 us (3%)
  between operations  0.64 us (2%)
    pallas_call x1, Pallas kernels, fused_device(): pl.pallas_call(functools.partial(kernel, groups, banks, members), out_sha...  38.8 us
    unnamed x2, local copies, waits for them, and re-layouts  1.42 us

profile of v3, /device:TPU:0, one launch (start us, length us, event | category | flops | bytes accessed | tf_op | source)
XLA Modules:
  0.0 40.9 jit_solution(14491386514765630334)
XLA Ops:
  0.6 38.8 %shard_map.68 = (bf16[8,4096]{1,0:T(8,128)(2,1)S(1)}, f32[4,32768]{1,0:T(4,128)S(1)}) custom-call(bf16[4,32768]{1,0:T(4,128)(2,1)} %density_hbm.1, s32[4]{0:T(128)} %label_hbm.1, bf16[4,1024,256]{2,1,0:T(8,128)(2,1)} %constant.6.clone.pair_hbm, bf16[128,384]{1,0:T(8,128)(2,1)} %constant.7.clone.line_hbm, f32[136,128]{1,0:T(8,128)} %constant.8.clone.scale_hbm), custom_call_target="tpu_custom_call" | custom-call | tf_op jit(solution)/shard_map/pallas_call | solution.py:237
  39.4 0.6 %copy.9 = bf16[8,4096]{1,0:T(8,128)(2,1)} copy(bf16[8,4096]{1,0:T(8,128)(2,1)S(1)} %get-tuple-element.4) | data formatting | bytes 131072
  40.1 0.8 %copy.10 = f32[4,32768]{1,0:T(4,128)} copy(f32[4,32768]{1,0:T(4,128)S(1)} %get-tuple-element.5) | data formatting | bytes 1048576

commit v4 on v3

--- a/solution.py
+++ b/solution.py
@@ -30,7 +30,7 @@
     groups, banks, members,
     density_hbm, label_hbm, pair_hbm, line_hbm, scale_hbm,
     centers_ref, potential_ref,
-    density_ref, label_ref, line_ref, scale_ref, pair, raised, source, lifted, smoothed, outgoing, incoming, partial, partial_in, shared, chosen, chosen_in,
+    density_ref, label_ref, line_ref, scale_ref, pair, source, running, lifted, smoothed, outgoing, incoming, partial, partial_in, shared, chosen, chosen_in,
     labels, label_out, count_out, count_in,
     load_sem, label_sem, count_sem, member_send, member_recv, partial_sem, shared_send, shared_recv, chosen_send, chosen_recv,
 ):
@@ -81,10 +81,12 @@
     loads = [
         pltpu.make_async_copy(src, dst, load_sem.at[index])
         for index, (src, dst) in enumerate((
-            (density_hbm, density_ref), (label_hbm, label_ref), (scale_hbm, scale_ref),
-            (line_hbm, line_ref), (pair_hbm, pair),
+            (density_hbm, density_ref), (label_hbm, label_ref), (scale_hbm, scale_ref), (line_hbm, line_ref),
         ))
     ]
+    for step in range(groups):
+        tile = tile_at(step)
+        loads.append(pltpu.make_async_copy(pair_hbm.at[tile], pair.at[tile], load_sem.at[4 + step]))
     for load in loads:
         load.start()
     barrier = pltpu.get_barrier_semaphore()
@@ -116,10 +118,8 @@
             scale = scale_ref[:rows, :] * scale_ref[rows + column:rows + column + 1, :]
             source[:, column * 128:(column + 1) * 128] = (risen[:, part * 128:(part + 1) * 128] * scale).astype(BF16)
     loads[3].wait()
-    loads[4].wait()
-
-    def convolve(field, tile):
-        inner = jnp.dot(field, pair[tile], preferred_element_type=F32)
+
+    def across(inner):
         high = inner.astype(BF16)
         low = (inner - high.astype(F32)).astype(BF16)
         return jnp.dot(line_ref[...], jnp.concatenate([high, high, low], axis=0), preferred_element_type=F32)
@@ -127,20 +127,19 @@
     pick = None
     for iteration in range(ITERS):
         last = iteration == ITERS - 1
-        if iteration:
-            for tile in range(groups):
-                source[:, tile * width:(tile + 1) * width] = (lifted[tile] / convolve(raised[...], tile)).astype(BF16)
-
         for step in range(groups):
             tile = tile_at(step)
-            value = jnp.log(convolve(source[...], tile))
+            if iteration == 0:
+                loads[4 + step].wait()
+            value = jnp.log(across(jnp.dot(source[...], pair[tile], preferred_element_type=F32)))
             smoothed[tile] = value
             outgoing[iteration, tile] = value.astype(BF16)
             if iteration == 0 and step == 0:
                 pl.semaphore_wait(barrier, banks - 1 + groups - 1)
+            spread(outgoing, incoming, iteration, tile, member_send, member_recv)
+            if iteration == 0 and step == 0:
                 for hop in range(1, banks):
                     push(label_out, labels.at[chunk_at(bank), :], label_sem.at[0], label_sem.at[1], (blk, bank_at(hop)))
-            spread(outgoing, incoming, iteration, tile, member_send, member_recv)
 
         if iteration == 0:
             await_bytes(labels.at[0:rows - chunk, :], label_sem.at[1])
@@ -204,7 +203,17 @@
                     start = pl.multiple_of(x * PLANE + tile * width, width)
                     potential_ref[:, pl.ds(start, width)] = value[members * x:members * (x + 1), :]
             else:
-                raised[:, pl.ds(pl.multiple_of(tile * width, width), width)] = jnp.exp(value).astype(BF16)
+                raised = jnp.exp(value).astype(BF16)
+                depth = pl.ds(pl.multiple_of(tile * width, width), width)
+                for target in range(groups):
+                    inner = jnp.dot(raised, pair[target, depth, :], preferred_element_type=F32)
+                    if step < groups - 1:
+                        inner += running[target]
+                    if step:
+                        running[target] = inner
+                    else:
+                        columns = slice(target * width, (target + 1) * width)
+                        source[:, columns] = (lifted[target] / across(inner)).astype(BF16)
 
     for _ in range(banks - 1):
         await_bytes(label_out, label_sem.at[0])
@@ -215,6 +224,17 @@
         await_bytes(partial.at[iteration, 0:groups - 1], partial_sem.at[iteration, 0])
         await_bytes(shared.at[iteration, 0:groups - 1], shared_send.at[iteration])
         await_bytes(chosen.at[iteration, :, 0:rows - chunk, :], chosen_send.at[iteration])
+
+
+def store_results(centers_in, potential_in, centers_out, potential_out, sems):
+    copies = [
+        pltpu.make_async_copy(centers_in, centers_out, sems.at[0]),
+        pltpu.make_async_copy(potential_in, potential_out, sems.at[1]),
+    ]
+    for copy in copies:
+        copy.start()
+    for copy in copies:
+        copy.wait()
 
 
 def fused_device(groups, banks, log_density, assignment):
@@ -234,7 +254,7 @@
     operands = (log_density, assignment, jnp.asarray(tiled_pair), jnp.asarray(line_parts), jnp.asarray(scales))
     vmem = pl.BlockSpec(memory_space=pltpu.VMEM)
     dma = pltpu.SemaphoreType.DMA
-    return pl.pallas_call(
+    results = pl.pallas_call(
         functools.partial(kernel, groups, banks, members),
         out_shape=(
             jax.ShapeDtypeStruct((BARS, cells // banks), BF16),
@@ -249,7 +269,7 @@
             pltpu.VMEM(scales.shape, F32),
             pltpu.VMEM((groups, PLANE, width), BF16),
             pltpu.VMEM((rows, PLANE), BF16),
-            pltpu.VMEM((rows, PLANE), BF16),
+            pltpu.VMEM((groups, rows, width), F32),
             pltpu.VMEM((groups, rows, width), F32),
             pltpu.VMEM((groups, rows, width), F32),
             pltpu.VMEM((ITERS, groups, rows, width), BF16),
@@ -263,7 +283,7 @@
             pltpu.VMEM((chunk, 128), BF16),
             pltpu.VMEM((BARS, 128), F32),
             pltpu.VMEM((groups, BARS, 128), F32),
-            dma((5,)), dma((2,)), dma((2,)),
+            dma((4 + groups,)), dma((2,)), dma((2,)),
             dma((ITERS,)), dma((ITERS, groups)),
             dma((ITERS, 2)),
             dma((ITERS,)), dma((ITERS, groups)),
@@ -273,6 +293,13 @@
             collective_id=0, has_side_effects=True, vmem_limit_bytes=40 * 1024 * 1024
         ),
     )(*(pltpu.with_memory_space_constraint(operand, pltpu.HBM) for operand in operands))
+    return pl.pallas_call(
+        store_results,
+        out_shape=tuple(jax.ShapeDtypeStruct(result.shape, result.dtype) for result in results),
+        in_specs=[pl.BlockSpec(memory_space=pl.ANY)] * 2,
+        out_specs=(pl.BlockSpec(memory_space=pl.ANY),) * 2,
+        scratch_shapes=[dma((2,))],
+    )(*results)
 
 
 def log_convolve(field_log, kernel_line, kernel_pair):

time: 41 us -> 59.9 us (1.46)
  Pallas kernels: 38.8 us -> 57.7 us
    pallas_call x0 -> x1, Pallas kernels: none -> 19 us  [fused_device(): pl.pallas_call(store_results, out_shape=tuple((jax.ShapeDtypeStruct(resul...]
    unnamed x2 -> x4, local copies, waits for them, and re-layouts: 1.42 us -> 1.41 us
where the time goes in v4:
time: 59.9 us; the launch traced here: 59.8 us
  Pallas kernels  57.7 us (96%)
  local copies, waits for them, and re-layouts  1.41 us (2%)
  between operations  0.65 us (1%)
    pallas_call x1, Pallas kernels, fused_device(): pl.pallas_call(functools.partial(kernel, groups, banks, members), out_sha...  38.8 us
    pallas_call x1, Pallas kernels, fused_device(): pl.pallas_call(store_results, out_shape=tuple((jax.ShapeDtypeStruct(resul...  19 us
    unnamed x4, local copies, waits for them, and re-layouts  1.41 us

profile of v4, /device:TPU:0, one launch (start us, length us, event | category | flops | bytes accessed | tf_op | source)
XLA Modules:
  0.0 59.8 jit_solution(8472297791973582283)
XLA Ops:
  0.6 38.8 %shard_map.68 = (bf16[8,4096]{1,0:T(8,128)(2,1)S(1)}, f32[4,32768]{1,0:T(4,128)S(1)}) custom-call(bf16[4,32768]{1,0:T(4,128)(2,1)} %density_hbm.1, s32[4]{0:T(128)} %label_hbm.1, bf16[4,1024,256]{2,1,0:T(8,128)(2,1)} %constant.6.clone.pair_hbm, bf16[128,384]{1,0:T(8,128)(2,1)} %constant.7.clone.line_hbm, f32[136,128]{1,0:T(8,128)} %constant.8.clone.scale_hbm), custom_call_target="tpu_custom_call" | custom-call | tf_op jit(solution)/shard_map/pallas_call | solution.py:257
  39.4 0.0 copy-start
  39.4 0.8 %copy-done = f32[4,32768]{1,0:T(4,128)} copy-done((f32[4,32768]{1,0:T(4,128)}, f32[4,32768]{1,0:T(4,128)S(1)}, u32[]{:S(2)}) %copy-start) | copy-done | bytes 524312
  40.2 0.0 copy-start.1
  40.2 0.6 %copy-done.1 = bf16[8,4096]{1,0:T(8,128)(2,1)} copy-done((bf16[8,4096]{1,0:T(8,128)(2,1)}, bf16[8,4096]{1,0:T(8,128)(2,1)S(1)}, u32[]{:S(2)}) %copy-start.1) | copy-done | bytes 65560
  40.8 19.0 %shard_map.69 = (bf16[8,4096]{1,0:T(8,128)(2,1)}, f32[4,32768]{1,0:T(4,128)}) custom-call(bf16[8,4096]{1,0:T(8,128)(2,1)} %copy-done.1, f32[4,32768]{1,0:T(4,128)} %copy-done), custom_call_target="tpu_custom_call" | custom-call | tf_op jit(solution)/shard_map/pallas_call | solution.py:296
Async XLA Ops:
  39.4 0.8 %copy-start = (f32[4,32768]{1,0:T(4,128)}, f32[4,32768]{1,0:T(4,128)S(1)}, u32[]{:S(2)}) copy-start(f32[4,32768]{1,0:T(4,128)S(1)} %get-tuple-element.5.potential_in) | copy-start | bytes 1572868
  40.2 0.6 %copy-start.1 = (bf16[8,4096]{1,0:T(8,128)(2,1)}, bf16[8,4096]{1,0:T(8,128)(2,1)S(1)}, u32[]{:S(2)}) copy-start(bf16[8,4096]{1,0:T(8,128)(2,1)S(1)} %get-tuple-element.4.centers_in) | copy-start | bytes 196612

commit v5 on v4

--- a/solution.py
+++ b/solution.py
@@ -44,8 +44,17 @@
     def group_at(step):
         return lax.rem(blk + step, groups)
 
-    def bank_at(step):
-        return lax.rem(bank + step, banks)
+    order = sorted(range(1, banks), key=lambda mask: ((mask == 1) * 4 + (mask // 2 == 1) * 2 + mask % 2, -mask))
+    folds = banks & (banks - 1) == 0
+
+    def bank_at(hop):
+        if not folds:
+            return lax.rem(bank + hop, banks)
+        peer, bit = 0, 1
+        while bit < banks:
+            peer += lax.rem(bank // bit + order[hop - 1] // bit, 2) * bit
+            bit *= 2
+        return peer
 
     def chunk_at(index):
         return pl.ds(pl.multiple_of(index * chunk, chunk), chunk)
@@ -172,10 +181,10 @@
         if iteration == 0:
             await_bytes(count_in.at[0:groups - 1], count_sem.at[1])
             counts = functools.reduce(jnp.add, [count_in[group] for group in range(groups)])
-            counts = jnp.concatenate([counts[:, :1]] * slabs, axis=0)
+            scale = 1.0 / jnp.concatenate([counts[:, :1]] * slabs, axis=0)
         await_bytes(partial_in.at[iteration, 0:groups - 1], partial_sem.at[iteration, 1])
         total = functools.reduce(jnp.add, [partial_in[iteration, group] for group in range(groups)])
-        shared[iteration, blk] = (total / counts).astype(BF16)
+        shared[iteration, blk] = (total * scale).astype(BF16)
         for step in range(groups - 1):
             push(
                 shared.at[iteration, blk], shared.at[iteration, blk],
@@ -189,10 +198,11 @@
             center = shared[iteration, tile]
             chosen[iteration, tile] = jnp.dot(pick, center, preferred_element_type=F32).astype(BF16)
             spread(chosen, chosen_in, iteration, tile, chosen_send, chosen_recv)
-            if last:
+        if last:
+            for tile in range(groups):
                 for slab in range(slabs):
-                    start = pl.multiple_of(slab * PLANE + tile * width, width)
-                    centers_ref[:, pl.ds(start, width)] = center[slab * BARS:(slab + 1) * BARS, :]
+                    start = slab * PLANE + tile * width
+                    centers_ref[:, start:start + width] = shared[iteration, tile, slab * BARS:(slab + 1) * BARS, :]
 
         for step in reversed(range(groups)):
             tile = tile_at(step)
@@ -293,13 +303,14 @@
             collective_id=0, has_side_effects=True, vmem_limit_bytes=40 * 1024 * 1024
         ),
     )(*(pltpu.with_memory_space_constraint(operand, pltpu.HBM) for operand in operands))
+    pinned = [pltpu.with_memory_space_constraint(result, pltpu.VMEM) for result in results]
     return pl.pallas_call(
         store_results,
-        out_shape=tuple(jax.ShapeDtypeStruct(result.shape, result.dtype) for result in results),
-        in_specs=[pl.BlockSpec(memory_space=pl.ANY)] * 2,
-        out_specs=(pl.BlockSpec(memory_space=pl.ANY),) * 2,
+        out_shape=tuple(pltpu.HBM(result.shape, result.dtype) for result in results),
+        in_specs=[vmem] * 2,
+        out_specs=(pl.BlockSpec(memory_space=pltpu.HBM),) * 2,
         scratch_shapes=[dma((2,))],
-    )(*results)
+    )(*pinned)
 
 
 def log_convolve(field_log, kernel_line, kernel_pair):

time: 59.9 us -> 40.4 us (0.67)
  Pallas kernels: 57.7 us -> 39.6 us
  local copies, waits for them, and re-layouts: 1.41 us -> 0 us
    pallas_call x1, Pallas kernels: 19 us -> 0.83 us  [fused_device(): pl.pallas_call(store_results, out_shape=tuple((pltpu.HBM(result.shape, re...]
    unnamed x4 -> x0, local copies, waits for them, and re-layouts: 1.41 us -> none
where the time goes in v5:
time: 40.4 us; the launch traced here: 40.3 us
  Pallas kernels  39.6 us (98%)
  between operations  0.64 us (2%)
    pallas_call x1, Pallas kernels, fused_device(): pl.pallas_call(functools.partial(kernel, groups, banks, members), out_sha...  38.8 us
    pallas_call x1, Pallas kernels, fused_device(): pl.pallas_call(store_results, out_shape=tuple((pltpu.HBM(result.shape, re...  0.83 us

profile of v5, /device:TPU:0, one launch (start us, length us, event | category | flops | bytes accessed | tf_op | source)
XLA Modules:
  0.0 40.3 jit_solution(9254076772570133034)
XLA Ops:
  0.6 38.8 %shard_map.68 = (bf16[8,4096]{1,0:T(8,128)(2,1)S(1)}, f32[4,32768]{1,0:T(4,128)S(1)}) custom-call(bf16[4,32768]{1,0:T(4,128)(2,1)} %density_hbm.1, s32[4]{0:T(128)} %label_hbm.1, bf16[4,1024,256]{2,1,0:T(8,128)(2,1)} %constant.6.clone.pair_hbm, bf16[128,384]{1,0:T(8,128)(2,1)} %constant.7.clone.line_hbm, f32[136,128]{1,0:T(8,128)} %constant.8.clone.scale_hbm), custom_call_target="tpu_custom_call" | custom-call | tf_op jit(solution)/shard_map/pallas_call | solution.py:267
  39.4 0.8 %shard_map.69 = (bf16[8,4096]{1,0:T(8,128)(2,1)}, f32[4,32768]{1,0:T(4,128)}) custom-call(bf16[8,4096]{1,0:T(8,128)(2,1)S(1)} %get-tuple-element.4.centers_in, f32[4,32768]{1,0:T(4,128)S(1)} %get-tuple-element.5.potential_in), custom_call_target="tpu_custom_call" | custom-call | tf_op jit(solution)/shard_map/pallas_call | solution.py:307

commit v6 on v5

--- a/solution.py
+++ b/solution.py
@@ -30,9 +30,9 @@
     groups, banks, members,
     density_hbm, label_hbm, pair_hbm, line_hbm, scale_hbm,
     centers_ref, potential_ref,
-    density_ref, label_ref, line_ref, scale_ref, pair, source, running, lifted, smoothed, outgoing, incoming, partial, partial_in, shared, chosen, chosen_in,
+    density_ref, label_ref, line_ref, scale_ref, pair, source, running, lifted, smoothed, outgoing, incoming, partial, shared, chosen, chosen_in,
     labels, label_out, count_out, count_in,
-    load_sem, label_sem, count_sem, member_send, member_recv, partial_sem, shared_send, shared_recv, chosen_send, chosen_recv,
+    load_sem, label_sem, count_sem, member_send, member_recv, partial_send, partial_recv, chosen_send, chosen_recv,
 ):
     blk, bank = lax.axis_index("blk"), lax.axis_index("bank")
     rows = G * members
@@ -40,9 +40,6 @@
     slabs = G // banks
     width = PLANE // groups
     kept = slabs * BARS
-
-    def group_at(step):
-        return lax.rem(blk + step, groups)
 
     order = sorted(range(1, banks), key=lambda mask: ((mask == 1) * 4 + (mask // 2 == 1) * 2 + mask % 2, -mask))
     folds = banks & (banks - 1) == 0
@@ -59,9 +56,7 @@
     def chunk_at(index):
         return pl.ds(pl.multiple_of(index * chunk, chunk), chunk)
 
-    def tile_at(step):
-        if step == groups - 1:
-            return blk
+    def group_at(step):
         up = step + (blk <= step).astype(jnp.int32)
         down = groups - 1 - step - (groups - 1 - blk <= step).astype(jnp.int32)
         return jnp.where(2 * blk >= groups, up, down)
@@ -87,23 +82,21 @@
     def await_bytes(ref, sem):
         pltpu.make_async_copy(ref, ref, sem).wait()
 
+    barrier = pltpu.get_barrier_semaphore()
+    for step in range(groups - 1):
+        pl.semaphore_signal(barrier, inc=1, device_id=(group_at(step), bank), device_id_type=MESH)
+    for hop in range(1, banks):
+        pl.semaphore_signal(barrier, inc=1, device_id=(blk, bank_at(hop)), device_id_type=MESH)
     loads = [
         pltpu.make_async_copy(src, dst, load_sem.at[index])
         for index, (src, dst) in enumerate((
             (density_hbm, density_ref), (label_hbm, label_ref), (scale_hbm, scale_ref), (line_hbm, line_ref),
         ))
     ]
-    for step in range(groups):
-        tile = tile_at(step)
-        loads.append(pltpu.make_async_copy(pair_hbm.at[tile], pair.at[tile], load_sem.at[4 + step]))
+    for tile in range(groups):
+        loads.append(pltpu.make_async_copy(pair_hbm.at[tile], pair.at[tile], load_sem.at[4 + tile]))
     for load in loads:
         load.start()
-    barrier = pltpu.get_barrier_semaphore()
-    for step in range(1, banks):
-        pl.semaphore_signal(barrier, inc=1, device_id=(blk, bank_at(step)), device_id_type=MESH)
-    for step in range(1, groups):
-        pl.semaphore_signal(barrier, inc=1, device_id=(group_at(step), bank), device_id_type=MESH)
-
     loads[1].wait()
     own_rows = lax.broadcasted_iota(jnp.int32, (chunk, 128), 0) % members
     own_labels = jnp.zeros((chunk, 128), F32)
@@ -136,17 +129,16 @@
     pick = None
     for iteration in range(ITERS):
         last = iteration == ITERS - 1
-        for step in range(groups):
-            tile = tile_at(step)
+        for tile in range(groups):
             if iteration == 0:
-                loads[4 + step].wait()
+                loads[4 + tile].wait()
             value = jnp.log(across(jnp.dot(source[...], pair[tile], preferred_element_type=F32)))
             smoothed[tile] = value
             outgoing[iteration, tile] = value.astype(BF16)
-            if iteration == 0 and step == 0:
+            if iteration == 0 and tile == 0:
                 pl.semaphore_wait(barrier, banks - 1 + groups - 1)
             spread(outgoing, incoming, iteration, tile, member_send, member_recv)
-            if iteration == 0 and step == 0:
+            if iteration == 0 and tile == 0:
                 for hop in range(1, banks):
                     push(label_out, labels.at[chunk_at(bank), :], label_sem.at[0], label_sem.at[1], (blk, bank_at(hop)))
 
@@ -162,64 +154,57 @@
             own_count = jnp.broadcast_to(jnp.sum(gather_wide[:BARS, :], axis=1, keepdims=True), (BARS, 128))
             count_out[...] = own_count
             count_in[blk] = own_count
-            for step in range(1, groups):
+            own_counts = jnp.concatenate([own_count[:, :1]] * slabs, axis=0)
+            for step in range(groups - 1):
                 push(count_out, count_in.at[blk], count_sem.at[0], count_sem.at[1], (group_at(step), bank))
 
-        for step in range(groups):
-            tile = tile_at(step)
+        for tile in range(groups):
             await_spread(incoming, iteration, tile, member_recv)
             sums = jnp.dot(gather, incoming[iteration, tile], preferred_element_type=F32)
-            if step < groups - 1:
-                partial[iteration, tile] = sums
+            if iteration:
+                sums -= own_counts * shared[iteration - 1, tile].astype(F32)
+            partial[iteration, tile, blk] = sums.astype(BF16)
+            for step in range(groups - 1):
                 push(
-                    partial.at[iteration, tile], partial_in.at[iteration, blk],
-                    partial_sem.at[iteration, 0], partial_sem.at[iteration, 1], (tile, bank),
+                    partial.at[iteration, tile, blk], partial.at[iteration, tile, blk],
+                    partial_send.at[iteration], partial_recv.at[iteration, tile], (group_at(step), bank),
                 )
-            else:
-                partial_in[iteration, blk] = sums
 
         if iteration == 0:
             await_bytes(count_in.at[0:groups - 1], count_sem.at[1])
             counts = functools.reduce(jnp.add, [count_in[group] for group in range(groups)])
             scale = 1.0 / jnp.concatenate([counts[:, :1]] * slabs, axis=0)
-        await_bytes(partial_in.at[iteration, 0:groups - 1], partial_sem.at[iteration, 1])
-        total = functools.reduce(jnp.add, [partial_in[iteration, group] for group in range(groups)])
-        shared[iteration, blk] = (total * scale).astype(BF16)
-        for step in range(groups - 1):
-            push(
-                shared.at[iteration, blk], shared.at[iteration, blk],
-                shared_send.at[iteration], shared_recv.at[iteration, blk], (tile_at(step), bank),
-            )
-
-        for step in reversed(range(groups)):
-            tile = tile_at(step)
-            if step < groups - 1:
-                await_bytes(shared.at[iteration, tile], shared_recv.at[iteration, tile])
-            center = shared[iteration, tile]
+        for tile in range(groups):
+            await_bytes(partial.at[iteration, tile, 0:groups - 1], partial_recv.at[iteration, tile])
+            total = functools.reduce(jnp.add, [partial[iteration, tile, group].astype(F32) for group in range(groups)])
+            center = total * scale
+            if iteration:
+                center += shared[iteration - 1, tile].astype(F32)
+            center = center.astype(BF16)
+            shared[iteration, tile] = center
             chosen[iteration, tile] = jnp.dot(pick, center, preferred_element_type=F32).astype(BF16)
             spread(chosen, chosen_in, iteration, tile, chosen_send, chosen_recv)
+
         if last:
             for tile in range(groups):
                 for slab in range(slabs):
                     start = slab * PLANE + tile * width
                     centers_ref[:, start:start + width] = shared[iteration, tile, slab * BARS:(slab + 1) * BARS, :]
 
-        for step in reversed(range(groups)):
-            tile = tile_at(step)
+        for tile in range(groups):
             await_spread(chosen_in, iteration, tile, chosen_recv)
             value = chosen_in[iteration, tile].astype(F32) - smoothed[tile]
             if last:
                 for x in range(G):
-                    start = pl.multiple_of(x * PLANE + tile * width, width)
-                    potential_ref[:, pl.ds(start, width)] = value[members * x:members * (x + 1), :]
+                    start = x * PLANE + tile * width
+                    potential_ref[:, start:start + width] = value[members * x:members * (x + 1), :]
             else:
                 raised = jnp.exp(value).astype(BF16)
-                depth = pl.ds(pl.multiple_of(tile * width, width), width)
                 for target in range(groups):
-                    inner = jnp.dot(raised, pair[target, depth, :], preferred_element_type=F32)
-                    if step < groups - 1:
+                    inner = jnp.dot(raised, pair[target, tile * width:(tile + 1) * width, :], preferred_element_type=F32)
+                    if tile:
                         inner += running[target]
-                    if step:
+                    if tile < groups - 1:
                         running[target] = inner
                     else:
                         columns = slice(target * width, (target + 1) * width)
@@ -231,8 +216,7 @@
         await_bytes(count_out, count_sem.at[0])
     for iteration in range(ITERS):
         await_bytes(outgoing.at[iteration, :, 0:rows - chunk, :], member_send.at[iteration])
-        await_bytes(partial.at[iteration, 0:groups - 1], partial_sem.at[iteration, 0])
-        await_bytes(shared.at[iteration, 0:groups - 1], shared_send.at[iteration])
+        await_bytes(partial.at[iteration, :, 0:groups - 1], partial_send.at[iteration])
         await_bytes(chosen.at[iteration, :, 0:rows - chunk, :], chosen_send.at[iteration])
 
 
@@ -284,8 +268,7 @@
             pltpu.VMEM((groups, rows, width), F32),
             pltpu.VMEM((ITERS, groups, rows, width), BF16),
             pltpu.VMEM((ITERS, groups, rows, width), BF16),
-            pltpu.VMEM((ITERS, groups, kept, width), F32),
-            pltpu.VMEM((ITERS, groups, kept, width), F32),
+            pltpu.VMEM((ITERS, groups, groups, kept, width), BF16),
             pltpu.VMEM((ITERS, groups, kept, width), BF16),
             pltpu.VMEM((ITERS, groups, rows, width), BF16),
             pltpu.VMEM((ITERS, groups, rows, width), BF16),
@@ -295,7 +278,6 @@
             pltpu.VMEM((groups, BARS, 128), F32),
             dma((4 + groups,)), dma((2,)), dma((2,)),
             dma((ITERS,)), dma((ITERS, groups)),
-            dma((ITERS, 2)),
             dma((ITERS,)), dma((ITERS, groups)),
             dma((ITERS,)), dma((ITERS, groups)),
         ],

time: 40.4 us -> 38.5 us (0.953)
  Pallas kernels: 39.6 us -> 37.7 us
    pallas_call x1, Pallas kernels: 38.8 us -> 36.9 us  [fused_device(): pl.pallas_call(functools.partial(kernel, groups, banks, members), out_sha...]
where the time goes in v6:
time: 38.5 us; the launch traced here: 38.4 us
  Pallas kernels  37.7 us (98%)
  between operations  0.64 us (2%)
    pallas_call x1, Pallas kernels, fused_device(): pl.pallas_call(functools.partial(kernel, groups, banks, members), out_sha...  36.9 us
    pallas_call x1, Pallas kernels, fused_device(): pl.pallas_call(store_results, out_shape=tuple((pltpu.HBM(result.shape, re...  0.83 us

profile of v6, /device:TPU:0, one launch (start us, length us, event | category | flops | bytes accessed | tf_op | source)
XLA Modules:
  0.0 38.4 jit_solution(16570024512128416665)
XLA Ops:
  0.6 36.9 %shard_map.68 = (bf16[8,4096]{1,0:T(8,128)(2,1)S(1)}, f32[4,32768]{1,0:T(4,128)S(1)}) custom-call(bf16[4,32768]{1,0:T(4,128)(2,1)} %density_hbm.1, s32[4]{0:T(128)} %label_hbm.1, bf16[4,1024,256]{2,1,0:T(8,128)(2,1)} %constant.6.clone.pair_hbm, bf16[128,384]{1,0:T(8,128)(2,1)} %constant.7.clone.line_hbm, f32[136,128]{1,0:T(8,128)} %constant.8.clone.scale_hbm), custom_call_target="tpu_custom_call" | custom-call | tf_op jit(solution)/shard_map/pallas_call | solution.py:251
  37.5 0.8 %shard_map.69 = (bf16[8,4096]{1,0:T(8,128)(2,1)}, f32[4,32768]{1,0:T(4,128)}) custom-call(bf16[8,4096]{1,0:T(8,128)(2,1)S(1)} %get-tuple-element.4.centers_in, f32[4,32768]{1,0:T(4,128)S(1)} %get-tuple-element.5.potential_in), custom_call_target="tpu_custom_call" | custom-call | tf_op jit(solution)/shard_map/pallas_call | solution.py:289

commit v7 on v6

--- a/solution.py
+++ b/solution.py
@@ -30,9 +30,9 @@
     groups, banks, members,
     density_hbm, label_hbm, pair_hbm, line_hbm, scale_hbm,
     centers_ref, potential_ref,
-    density_ref, label_ref, line_ref, scale_ref, pair, source, running, lifted, smoothed, outgoing, incoming, partial, shared, chosen, chosen_in,
+    density_ref, label_ref, line_ref, scale_ref, pair, source, running, lifted, smoothed, outgoing, incoming, partial, shared, shared_in, chosen, chosen_in,
     labels, label_out, count_out, count_in,
-    load_sem, label_sem, count_sem, member_send, member_recv, partial_send, partial_recv, chosen_send, chosen_recv,
+    load_sem, label_sem, count_sem, shared_sem, member_send, member_recv, partial_send, partial_recv, chosen_send, chosen_recv,
 ):
     blk, bank = lax.axis_index("blk"), lax.axis_index("bank")
     rows = G * members
@@ -45,6 +45,8 @@
     folds = banks & (banks - 1) == 0
 
     def bank_at(hop):
+        if hop == 0:
+            return bank
         if not folds:
             return lax.rem(bank + hop, banks)
         peer, bit = 0, 1
@@ -56,22 +58,47 @@
     def chunk_at(index):
         return pl.ds(pl.multiple_of(index * chunk, chunk), chunk)
 
+    side = lax.rem(blk, 2)
+    pair_at = blk // 2
+    pairs = groups // 2
+    facing = blk + 1 - 2 * side
+
+    def own_tile(index):
+        return side * pairs + index
+
+    def facing_tile(index):
+        return (1 - side) * pairs + index
+
+    def tile_at(step):
+        return own_tile(step // 2) if step % 2 else facing_tile(step // 2)
+
+    def partner_at(step):
+        return lax.rem(blk + 2 * step, groups)
+
+    order = sorted(range(1, banks), key=lambda mask: ((mask == 1) * 4 + (mask // 2 == 1) * 2 + mask % 2, -mask))
+    folds = banks & (banks - 1) == 0
+
+    def bank_at(hop):
+        if hop == 0:
+            return bank
+        if not folds:
+            return lax.rem(bank + hop, banks)
+        peer, bit = 0, 1
+        while bit < banks:
+            peer += lax.rem(bank // bit + order[hop - 1] // bit, 2) * bit
+            bit *= 2
+        return peer
+
+    def chunk_at(index):
+        return pl.ds(pl.multiple_of(index * chunk, chunk), chunk)
+
     def group_at(step):
         up = step + (blk <= step).astype(jnp.int32)
         down = groups - 1 - step - (groups - 1 - blk <= step).astype(jnp.int32)
         return jnp.where(2 * blk >= groups, up, down)
 
-    def spread(src, dst, iteration, tile, send_sem, recv_sem):
-        for hop in range(1, banks):
-            peer = bank_at(hop)
-            push(
-                src.at[iteration, tile, chunk_at(peer), :], dst.at[iteration, tile, chunk_at(bank), :],
-                send_sem.at[iteration], recv_sem.at[iteration, tile], (blk, peer),
-            )
-        dst[iteration, tile, chunk_at(bank), :] = src[iteration, tile, chunk_at(bank), :]
-
-    def await_spread(dst, iteration, tile, recv_sem):
-        await_bytes(dst.at[iteration, tile, 0:rows - chunk, :], recv_sem.at[iteration, tile])
+    def chunk_of(plane_side, index):
+        return pl.ds(pl.multiple_of(plane_side * rows + index * chunk, chunk), chunk)
 
     def push(src, dst, send_sem, recv_sem, device):
         pltpu.make_async_remote_copy(
@@ -83,8 +110,10 @@
         pltpu.make_async_copy(ref, ref, sem).wait()
 
     barrier = pltpu.get_barrier_semaphore()
-    for step in range(groups - 1):
-        pl.semaphore_signal(barrier, inc=1, device_id=(group_at(step), bank), device_id_type=MESH)
+    for hop in range(banks):
+        pl.semaphore_signal(barrier, inc=1, device_id=(facing, bank_at(hop)), device_id_type=MESH)
+    for step in range(1, pairs):
+        pl.semaphore_signal(barrier, inc=1, device_id=(partner_at(step), bank), device_id_type=MESH)
     for hop in range(1, banks):
         pl.semaphore_signal(barrier, inc=1, device_id=(blk, bank_at(hop)), device_id_type=MESH)
     loads = [
@@ -93,8 +122,9 @@
             (density_hbm, density_ref), (label_hbm, label_ref), (scale_hbm, scale_ref), (line_hbm, line_ref),
         ))
     ]
-    for tile in range(groups):
-        loads.append(pltpu.make_async_copy(pair_hbm.at[tile], pair.at[tile], load_sem.at[4 + tile]))
+    for step in range(groups):
+        tile = tile_at(step)
+        loads.append(pltpu.make_async_copy(pair_hbm.at[tile], pair.at[tile], load_sem.at[4 + step]))
     for load in loads:
         load.start()
     loads[1].wait()
@@ -103,7 +133,7 @@
     for member in range(members):
         own_labels = jnp.where(own_rows == member, label_ref[member].astype(F32), own_labels)
     label_out[...] = own_labels.astype(BF16)
-    labels[chunk_at(bank), :] = own_labels.astype(BF16)
+    labels[chunk_of(side, bank), :] = own_labels.astype(BF16)
 
     loads[0].wait()
     for tile in range(groups):
@@ -129,23 +159,37 @@
     pick = None
     for iteration in range(ITERS):
         last = iteration == ITERS - 1
-        for tile in range(groups):
+        for step in range(groups):
+            tile = tile_at(step)
             if iteration == 0:
-                loads[4 + tile].wait()
+                loads[4 + step].wait()
             value = jnp.log(across(jnp.dot(source[...], pair[tile], preferred_element_type=F32)))
             smoothed[tile] = value
             outgoing[iteration, tile] = value.astype(BF16)
-            if iteration == 0 and tile == 0:
-                pl.semaphore_wait(barrier, banks - 1 + groups - 1)
-            spread(outgoing, incoming, iteration, tile, member_send, member_recv)
-            if iteration == 0 and tile == 0:
-                for hop in range(1, banks):
-                    push(label_out, labels.at[chunk_at(bank), :], label_sem.at[0], label_sem.at[1], (blk, bank_at(hop)))
+            if iteration == 0 and step == 0:
+                pl.semaphore_wait(barrier, 2 * banks - 1 + pairs - 1)
+            own = step % 2
+            for hop in range(own, banks):
+                peer = bank_at(hop)
+                push(
+                    outgoing.at[iteration, tile, chunk_at(peer), :],
+                    incoming.at[iteration, step // 2, chunk_of(side, bank), :],
+                    member_send.at[iteration], member_recv.at[iteration, step // 2], (blk if own else facing, peer),
+                )
+            if own:
+                incoming[iteration, step // 2, chunk_of(side, bank), :] = outgoing[iteration, tile, chunk_at(bank), :]
+            if iteration == 0 and step == 0:
+                for plane, start in ((facing, 0), (blk, 1)):
+                    for hop in range(start, banks):
+                        push(
+                            label_out, labels.at[chunk_of(side, bank), :],
+                            label_sem.at[0], label_sem.at[1], (plane, bank_at(hop)),
+                        )
 
         if iteration == 0:
-            await_bytes(labels.at[0:rows - chunk, :], label_sem.at[1])
-            row = lax.broadcasted_iota(jnp.int32, (rows, 128), 0)
-            lane = lax.broadcasted_iota(jnp.int32, (rows, 128), 1)
+            await_bytes(labels.at[0:2 * rows - chunk, :], label_sem.at[1])
+            row = lax.broadcasted_iota(jnp.int32, (2 * rows, 128), 0)
+            lane = lax.broadcasted_iota(jnp.int32, (2 * rows, 128), 1)
             match = (labels[...].astype(F32) == (lane % BARS).astype(F32)) & ((row // members) % slabs == lane // BARS)
             pick_wide = jnp.where(match, 1.0, 0.0).astype(F32)
             gather_wide = jnp.transpose(pick_wide)
@@ -153,71 +197,88 @@
             gather = gather_wide.astype(BF16)[:kept, :]
             own_count = jnp.broadcast_to(jnp.sum(gather_wide[:BARS, :], axis=1, keepdims=True), (BARS, 128))
             count_out[...] = own_count
-            count_in[blk] = own_count
+            count_in[pair_at] = own_count
             own_counts = jnp.concatenate([own_count[:, :1]] * slabs, axis=0)
-            for step in range(groups - 1):
-                push(count_out, count_in.at[blk], count_sem.at[0], count_sem.at[1], (group_at(step), bank))
-
-        for tile in range(groups):
-            await_spread(incoming, iteration, tile, member_recv)
-            sums = jnp.dot(gather, incoming[iteration, tile], preferred_element_type=F32)
+            for step in range(1, pairs):
+                push(count_out, count_in.at[pair_at], count_sem.at[0], count_sem.at[1], (partner_at(step), bank))
+
+        for index in range(pairs):
+            await_bytes(incoming.at[iteration, index, 0:2 * rows - chunk, :], member_recv.at[iteration, index])
+            sums = jnp.dot(gather, incoming[iteration, index], preferred_element_type=F32)
             if iteration:
-                sums -= own_counts * shared[iteration - 1, tile].astype(F32)
-            partial[iteration, tile, blk] = sums.astype(BF16)
-            for step in range(groups - 1):
+                sums -= own_counts * shared[iteration - 1, index].astype(F32)
+            partial[iteration, index, pair_at] = sums.astype(BF16)
+            for step in range(1, pairs):
                 push(
-                    partial.at[iteration, tile, blk], partial.at[iteration, tile, blk],
-                    partial_send.at[iteration], partial_recv.at[iteration, tile], (group_at(step), bank),
+                    partial.at[iteration, index, pair_at], partial.at[iteration, index, pair_at],
+                    partial_send.at[iteration], partial_recv.at[iteration, index], (partner_at(step), bank),
                 )
 
         if iteration == 0:
-            await_bytes(count_in.at[0:groups - 1], count_sem.at[1])
-            counts = functools.reduce(jnp.add, [count_in[group] for group in range(groups)])
+            await_bytes(count_in.at[0:pairs - 1], count_sem.at[1])
+            counts = functools.reduce(jnp.add, [count_in[other] for other in range(pairs)])
             scale = 1.0 / jnp.concatenate([counts[:, :1]] * slabs, axis=0)
-        for tile in range(groups):
-            await_bytes(partial.at[iteration, tile, 0:groups - 1], partial_recv.at[iteration, tile])
-            total = functools.reduce(jnp.add, [partial[iteration, tile, group].astype(F32) for group in range(groups)])
+        for index in range(pairs):
+            await_bytes(partial.at[iteration, index, 0:pairs - 1], partial_recv.at[iteration, index])
+            total = functools.reduce(jnp.add, [partial[iteration, index, other].astype(F32) for other in range(pairs)])
             center = total * scale
             if iteration:
-                center += shared[iteration - 1, tile].astype(F32)
+                center += shared[iteration - 1, index].astype(F32)
             center = center.astype(BF16)
-            shared[iteration, tile] = center
-            chosen[iteration, tile] = jnp.dot(pick, center, preferred_element_type=F32).astype(BF16)
-            spread(chosen, chosen_in, iteration, tile, chosen_send, chosen_recv)
+            shared[iteration, index] = center
+            chosen[iteration, index] = jnp.dot(pick, center, preferred_element_type=F32).astype(BF16)
+            tile = own_tile(index)
+            for plane, plane_side, start in ((facing, 1 - side, 0), (blk, side, 1)):
+                for hop in range(start, banks):
+                    peer = bank_at(hop)
+                    push(
+                        chosen.at[iteration, index, chunk_of(plane_side, peer), :],
+                        chosen_in.at[iteration, tile, chunk_at(bank), :],
+                        chosen_send.at[iteration], chosen_recv.at[iteration, tile], (plane, peer),
+                    )
+            chosen_in[iteration, tile, chunk_at(bank), :] = chosen[iteration, index, chunk_of(side, bank), :]
+            if last:
+                push(shared.at[iteration, index], shared_in.at[index], shared_sem.at[0], shared_sem.at[1], (facing, bank))
 
         if last:
-            for tile in range(groups):
-                for slab in range(slabs):
-                    start = slab * PLANE + tile * width
-                    centers_ref[:, start:start + width] = shared[iteration, tile, slab * BARS:(slab + 1) * BARS, :]
-
-        for tile in range(groups):
-            await_spread(chosen_in, iteration, tile, chosen_recv)
+            await_bytes(shared_in, shared_sem.at[1])
+            for index in range(pairs):
+                for tile, found in ((own_tile(index), shared[iteration, index]), (facing_tile(index), shared_in[index])):
+                    for slab in range(slabs):
+                        start = pl.multiple_of(slab * PLANE + tile * width, width)
+                        centers_ref[:, pl.ds(start, width)] = found[slab * BARS:(slab + 1) * BARS, :]
+
+        for step in range(groups):
+            own = 1 - step % 2
+            tile = own_tile(step // 2) if own else facing_tile(step // 2)
+            await_bytes(chosen_in.at[iteration, tile, 0:rows - own * chunk, :], chosen_recv.at[iteration, tile])
             value = chosen_in[iteration, tile].astype(F32) - smoothed[tile]
             if last:
                 for x in range(G):
-                    start = x * PLANE + tile * width
-                    potential_ref[:, start:start + width] = value[members * x:members * (x + 1), :]
+                    start = pl.multiple_of(x * PLANE + tile * width, width)
+                    potential_ref[:, pl.ds(start, width)] = value[members * x:members * (x + 1), :]
             else:
                 raised = jnp.exp(value).astype(BF16)
+                depth = pl.ds(pl.multiple_of(tile * width, width), width)
                 for target in range(groups):
-                    inner = jnp.dot(raised, pair[target, tile * width:(tile + 1) * width, :], preferred_element_type=F32)
-                    if tile:
+                    inner = jnp.dot(raised, pair[target, depth, :], preferred_element_type=F32)
+                    if step:
                         inner += running[target]
-                    if tile < groups - 1:
+                    if step < groups - 1:
                         running[target] = inner
                     else:
                         columns = slice(target * width, (target + 1) * width)
                         source[:, columns] = (lifted[target] / across(inner)).astype(BF16)
 
-    for _ in range(banks - 1):
+    for _ in range(2 * banks - 1):
         await_bytes(label_out, label_sem.at[0])
-    for _ in range(groups - 1):
+    for _ in range(pairs - 1):
         await_bytes(count_out, count_sem.at[0])
+    await_bytes(shared_in, shared_sem.at[0])
     for iteration in range(ITERS):
-        await_bytes(outgoing.at[iteration, :, 0:rows - chunk, :], member_send.at[iteration])
-        await_bytes(partial.at[iteration, :, 0:groups - 1], partial_send.at[iteration])
-        await_bytes(chosen.at[iteration, :, 0:rows - chunk, :], chosen_send.at[iteration])
+        await_bytes(incoming.at[iteration, :, 0:2 * rows - chunk, :], member_send.at[iteration])
+        await_bytes(partial.at[iteration, :, 0:pairs - 1], partial_send.at[iteration])
+        await_bytes(chosen.at[iteration, :, 0:2 * rows - chunk, :], chosen_send.at[iteration])
 
 
 def store_results(centers_in, potential_in, centers_out, potential_out, sems):
@@ -235,6 +296,7 @@
     members, cells = log_density.shape
     rows, chunk = G * members, G * members // banks
     width = PLANE // groups
+    pairs = groups // 2
     kept = G // banks * BARS
     line, pair = host_tables()
     tiled_pair = np.ascontiguousarray(pair.reshape(PLANE, groups, width).transpose(1, 0, 2))
@@ -267,18 +329,19 @@
             pltpu.VMEM((groups, rows, width), F32),
             pltpu.VMEM((groups, rows, width), F32),
             pltpu.VMEM((ITERS, groups, rows, width), BF16),
+            pltpu.VMEM((ITERS, pairs, 2 * rows, width), BF16),
+            pltpu.VMEM((ITERS, pairs, pairs, kept, width), BF16),
+            pltpu.VMEM((ITERS, pairs, kept, width), BF16),
+            pltpu.VMEM((pairs, kept, width), BF16),
+            pltpu.VMEM((ITERS, pairs, 2 * rows, width), BF16),
             pltpu.VMEM((ITERS, groups, rows, width), BF16),
-            pltpu.VMEM((ITERS, groups, groups, kept, width), BF16),
-            pltpu.VMEM((ITERS, groups, kept, width), BF16),
-            pltpu.VMEM((ITERS, groups, rows, width), BF16),
-            pltpu.VMEM((ITERS, groups, rows, width), BF16),
-            pltpu.VMEM((rows, 128), BF16),
+            pltpu.VMEM((2 * rows, 128), BF16),
             pltpu.VMEM((chunk, 128), BF16),
             pltpu.VMEM((BARS, 128), F32),
-            pltpu.VMEM((groups, BARS, 128), F32),
-            dma((4 + groups,)), dma((2,)), dma((2,)),
-            dma((ITERS,)), dma((ITERS, groups)),
-            dma((ITERS,)), dma((ITERS, groups)),
+            pltpu.VMEM((pairs, BARS, 128), F32),
+            dma((4 + groups,)), dma((2,)), dma((2,)), dma((2,)),
+            dma((ITERS,)), dma((ITERS, pairs)),
+            dma((ITERS,)), dma((ITERS, pairs)),
             dma((ITERS,)), dma((ITERS, groups)),
         ],
         compiler_params=pltpu.CompilerParams(
@@ -334,7 +397,7 @@
     def per_device(log_density, assignment):
         rows = G * log_density.shape[0]
         fits = G % banks == 0 and (rows // banks) % 16 == 0 and PLANE % (128 * groups) == 0
-        if fits and min(groups, banks) > 1:
+        if fits and groups % 2 == 0 and groups > 2 and banks > 1:
             return fused_device(groups, banks, log_density, assignment)
         return plain_device(log_density, assignment)
 

time: 38.5 us -> 34.9 us (0.906)
  Pallas kernels: 37.7 us -> 34.1 us
    pallas_call x1, Pallas kernels: 36.9 us -> 33.2 us  [fused_device(): pl.pallas_call(functools.partial(kernel, groups, banks, members), out_sha...]
where the time goes in v7:
time: 34.9 us; the launch traced here: 34.7 us
  Pallas kernels  34.1 us (98%)
  between operations  0.64 us (2%)
    pallas_call x1, Pallas kernels, fused_device(): pl.pallas_call(functools.partial(kernel, groups, banks, members), out_sha...  33.2 us
    pallas_call x1, Pallas kernels, fused_device(): pl.pallas_call(store_results, out_shape=tuple((pltpu.HBM(result.shape, re...  0.83 us

profile of v7, /device:TPU:0, one launch (start us, length us, event | category | flops | bytes accessed | tf_op | source)
XLA Modules:
  0.0 34.7 jit_solution(3308464511640562669)
XLA Ops:
  0.6 33.2 %shard_map.68 = (bf16[8,4096]{1,0:T(8,128)(2,1)S(1)}, f32[4,32768]{1,0:T(4,128)S(1)}) custom-call(bf16[4,32768]{1,0:T(4,128)(2,1)} %density_hbm.1, s32[4]{0:T(128)} %label_hbm.1, bf16[4,1024,256]{2,1,0:T(8,128)(2,1)} %constant.6.clone.pair_hbm, bf16[128,384]{1,0:T(8,128)(2,1)} %constant.7.clone.line_hbm, f32[136,128]{1,0:T(8,128)} %constant.8.clone.scale_hbm), custom_call_target="tpu_custom_call" | custom-call | tf_op jit(solution)/shard_map/pallas_call | solution.py:313
  33.9 0.8 %shard_map.69 = (bf16[8,4096]{1,0:T(8,128)(2,1)}, f32[4,32768]{1,0:T(4,128)}) custom-call(bf16[8,4096]{1,0:T(8,128)(2,1)S(1)} %get-tuple-element.4.centers_in, f32[4,32768]{1,0:T(4,128)S(1)} %get-tuple-element.5.potential_in), custom_call_target="tpu_custom_call" | custom-call | tf_op jit(solution)/shard_map/pallas_call | solution.py:352

commit v8 on v7

--- a/solution.py
+++ b/solution.py
@@ -178,7 +178,7 @@
                 )
             if own:
                 incoming[iteration, step // 2, chunk_of(side, bank), :] = outgoing[iteration, tile, chunk_at(bank), :]
-            if iteration == 0 and step == 0:
+            if iteration == 0 and step == 1:
                 for plane, start in ((facing, 0), (blk, 1)):
                     for hop in range(start, banks):
                         push(

time: 34.9 us -> 35.1 us (level)
  no operation moved by 1% of the time
where the time goes in v8:
time: 35.1 us; the launch traced here: 35 us
  Pallas kernels  34.3 us (98%)
  between operations  0.64 us (2%)
    pallas_call x1, Pallas kernels, fused_device(): pl.pallas_call(functools.partial(kernel, groups, banks, members), out_sha...  33.5 us
    pallas_call x1, Pallas kernels, fused_device(): pl.pallas_call(store_results, out_shape=tuple((pltpu.HBM(result.shape, re...  0.83 us

profile of v8, /device:TPU:0, one launch (start us, length us, event | category | flops | bytes accessed | tf_op | source)
XLA Modules:
  0.0 35.0 jit_solution(2812376980074263652)
XLA Ops:
  0.6 33.5 %shard_map.68 = (bf16[8,4096]{1,0:T(8,128)(2,1)S(1)}, f32[4,32768]{1,0:T(4,128)S(1)}) custom-call(bf16[4,32768]{1,0:T(4,128)(2,1)} %density_hbm.1, s32[4]{0:T(128)} %label_hbm.1, bf16[4,1024,256]{2,1,0:T(8,128)(2,1)} %constant.6.clone.pair_hbm, bf16[128,384]{1,0:T(8,128)(2,1)} %constant.7.clone.line_hbm, f32[136,128]{1,0:T(8,128)} %constant.8.clone.scale_hbm), custom_call_target="tpu_custom_call" | custom-call | tf_op jit(solution)/shard_map/pallas_call | solution.py:313
  34.1 0.8 %shard_map.69 = (bf16[8,4096]{1,0:T(8,128)(2,1)}, f32[4,32768]{1,0:T(4,128)}) custom-call(bf16[8,4096]{1,0:T(8,128)(2,1)S(1)} %get-tuple-element.4.centers_in, f32[4,32768]{1,0:T(4,128)S(1)} %get-tuple-element.5.potential_in), custom_call_target="tpu_custom_call" | custom-call | tf_op jit(solution)/shard_map/pallas_call | solution.py:352
